TPU v7x, 256 devices: a whole 4x4x8 slice. The times are simulated.
256 devices in a mesh: runs: 8 (over z_lo, y), cells: 32 (over x, z_hi, core).
Axes of the slice: x: 4, y: 4, z: 8 (z_hi: 4, z_lo: 2; z = z_hi * 2 + z_lo), core: 2. Of those that a mesh axis runs over, the one named last changes fastest.
Arguments:
- fields: bfloat16 [64, 120, 65536], P('runs', None, 'cells'), may hold values from -100 to 100, as said below
- vectors: bfloat16 [64, 120, 48], P('runs'), may hold values from -1 to 1, as said below
- combos: bfloat16 [3072, 64], replicated, may hold values from -0.109375 to 0.109375
Outputs:
- gram: float32 [64, 120, 120], P('runs')
- basis: bfloat16 [3072, 65536], P('runs', 'cells')
- merged: float32 [3072, 3072], P('runs')
- eofs: bfloat16 [64, 65536], P(None, 'cells')
- pcs: float32 [64, 120, 64], P('runs')
Inputs may be any that keep to these rules, and one draw needn't show every extreme that they name: `fields`: each run shares a field with all others beside its own; the grid cells carry different scales. `vectors`: columns are not orthonormal.
All inputs are finite; a program needn't handle non-finite values.
Results may differ from a plain program's by a relative error of at most 0.0058.
Values may be sent and summed in bfloat16 or wider, within the bound.
No kernel may reach another device: no remote copies, remote signals or barrier semaphores. Data moves between devices by JAX's collectives and lax.ppermute only.
A program may use at most 64 MiB of HBM per device.

v0:
```python
import jax
import jax.numpy as jnp
from jax import lax
from jax.sharding import PartitionSpec as P


def per_device(fields, vectors, combos):
    run_dev, months, cells_dev = fields.shape
    modes = vectors.shape[2]
    total_cells = cells_dev * lax.axis_size("cells")
    rows_mine = run_dev * modes
    raw_gram = jnp.einsum("rmc,rnc->rmn", fields, fields, preferred_element_type=jnp.float32)
    projected = jnp.einsum("rmk,rmc->rkc", vectors, fields, preferred_element_type=jnp.float32)
    gram = lax.psum(raw_gram, "cells") / total_cells
    vec_wide = vectors.astype(jnp.float32)
    scale = jnp.einsum("rmk,rmn,rnk->rk", vec_wide, gram, vec_wide, precision=lax.Precision.HIGHEST)
    basis = (
        (projected / jnp.sqrt(scale)[:, :, None]).astype(jnp.bfloat16).reshape(rows_mine, cells_dev)
    )
    position = lax.axis_index("runs")
    weights_mine = lax.dynamic_slice_in_dim(combos, position * rows_mine, rows_mine, 0)
    everyone = lax.all_gather(basis, "runs", axis=0, tiled=True)
    partial_rows = lax.dot_general(
        basis, everyone, (((1,), (1,)), ((), ())), preferred_element_type=jnp.float32
    )
    merged = lax.psum(partial_rows, "cells") / total_cells
    mode_wide = lax.dot_general(
        combos, everyone, (((0,), (0,)), ((), ())), preferred_element_type=jnp.float32
    )
    mode = mode_wide.astype(jnp.bfloat16)
    projection = jnp.einsum("rmc,jc->rmj", fields, mode, preferred_element_type=jnp.float32)
    weighted = jnp.dot(merged, combos.astype(jnp.float32), precision=lax.Precision.HIGHEST)
    local_norms = jnp.sum(weights_mine.astype(jnp.float32) * weighted, axis=0)
    norms = lax.psum(local_norms, "runs")
    pcs_total = lax.psum(projection, "cells")
    root = jnp.sqrt(norms)
    eofs = (mode.astype(jnp.float32) / root[:, None]).astype(jnp.bfloat16)
    pcs = pcs_total / (total_cells * root)
    return (gram, basis, merged, eofs, pcs)


def solution(mesh):
    return jax.shard_map(
        per_device,
        mesh=mesh,
        in_specs=(P("runs", None, "cells"), P("runs", None, None), P()),
        out_specs=(
            P("runs", None, None),
            P("runs", "cells"),
            P("runs", None),
            P(None, "cells"),
            P("runs", None, None),
        ),
        check_vma=False,
    )
```

profile of v0, /device:TPU:1, one launch (start us, length us, event | category | flops | bytes accessed | tf_op | source)
XLA Modules:
  0.0 783.0 jit_solution(7843798936573000669)
XLA Ops:
  7.2 0.0 copy-start.6
  7.2 0.0 all-reduce.4.cloned.1.call-start
  7.2 5.3 fusion.3
  12.5 0.0 all-reduce.4.cloned.1.call-update
  12.5 0.0 all-gather.2.cloned.1.call-start
  12.6 282.9 %all-reduce.4.cloned.1.call-done = f32[8,120,120]{2,1,0:T(8,128)} async-done(((f32[8,120,120]{2,1,0:T(8,128)}), f32[8,120,120]{2,1,0:T(8,128)}) %all-reduce.4.cloned.1.call-update) | async-done | bytes 460816 | tf_op jit(solution)/shard_map/psum | solution.py:14
  295.5 1.1 broadcast_multiply_fusion.1
  296.6 0.0 copy-done.6
  296.6 0.0 copy-start.4
  296.6 0.6 convolution_bitcast_fusion
  297.2 0.2 copy.13
  297.4 0.1 multiply_reduce_fusion
  297.5 0.0 copy-start.3
  297.5 4.2 divide_convert_fusion
  301.7 0.0 copy-done.4
  301.7 0.0 all-gather.2.cloned.1.call-update
  301.7 0.0 all-reduce.6.cloned.1.call-start
  301.8 131.5 %all-gather.2.cloned.1.call-done = bf16[3072,2048]{1,0:T(8,128)(2,1)} async-done(((bf16[384,2048]{1,0:T(8,128)(2,1)}), bf16[3072,2048]{1,0:T(8,128)(2,1)}) %all-gather.2.cloned.1.call-update) | async-done | bytes 12582928 | tf_op jit(solution)/shard_map/all_gather | solution.py:22
  433.3 0.0 copy-done.3
  433.3 0.0 copy-start
  433.3 0.0 copy-start.1
  433.3 7.0 convolution_convert_fusion
  440.3 0.0 copy-done
  440.3 0.0 copy-start.5
  440.3 2.1 convolution_bitcast_fusion.1
  442.4 0.2 copy-done.1
  442.6 0.7 copy-done.5
  443.4 6.7 fusion.4
  450.1 0.0 all-reduce.6.cloned.1.call-update
  450.1 302.7 %all-reduce.6.cloned.1.call-done = (f32[384,3072]{1,0:T(8,128)}, f32[8,120,64]{1,2,0:T(8,128)}) async-done(((f32[384,3072]{1,0:T(8,128)}, f32[8,120,64]{1,2,0:T(8,128)}), (f32[384,3072]{1,0:T(8,128)}, f32[8,120,64]{1,2,0:T(8,128)})) %all-reduce.6.cloned.1.call-update) | async-done | bytes 4964368 | tf_op jit(solution)/shard_map/psum | solution.py:26
  752.8 2.9 broadcast_multiply_fusion
  755.7 0.0 copy-start.2
  755.7 2.2 copy-done.2
  757.9 0.0 copy-start.7
  757.9 2.6 fusion
  760.6 14.3 %psum.30 = f32[64]{0:T(128)S(1)} all-reduce(f32[64]{0:T(128)S(1)} %fusion), channel_id=1, replica_groups=mesh['runs'=8,'cells'=32] {'runs'}, use_global_device_ids=true, to_apply=%region_3.0 | all-reduce | flops 64 | bytes 512 | tf_op jit(solution)/shard_map/psum | solution.py:34
  774.9 0.8 fusion.1
  775.7 0.0 copy-done.7
  775.7 0.8 broadcast_divide_fusion
  (2 shorter events, 0.0 us)
Async XLA Ops:
  7.2 289.4 %copy-start.6 = (bf16[8,120,48]{1,2,0:T(8,128)(2,1)S(1)}, bf16[8,120,48]{1,2,0:T(8,128)(2,1)}, u32[]{:S(2)}) copy-start(bf16[8,120,48]{1,2,0:T(8,128)(2,1)} %param.4) | copy-start | bytes 276484
  7.2 288.3 %all-reduce.4.cloned.1.call-start = ((), (), s32[]{:S(2)}) async-start(), calls=%async_computation | async-start | bytes 983040 | tf_op jit(solution)/shard_map/psum | solution.py:14
  12.5 420.7 %all-gather.2.cloned.1.call-start = ((), (), s32[]{:S(2)}) async-start(), calls=%async_computation.1 | async-start | bytes 14155776 | tf_op jit(solution)/shard_map/all_gather | solution.py:22
  296.6 5.1 copy-start.4
  297.5 135.7 %copy-start.3 = (bf16[3072,64]{0,1:T(8,128)(2,1)S(1)}, bf16[3072,64]{0,1:T(8,128)(2,1)}, u32[]{:S(2)}) copy-start(bf16[3072,64]{0,1:T(8,128)(2,1)} %param.5) | copy-start | bytes 1179652
  301.7 451.1 %all-reduce.6.cloned.1.call-start = ((), (), s32[]{:S(2)}) async-start(), calls=%async_computation.2 | async-start | bytes 9961472 | tf_op jit(solution)/shard_map/psum | solution.py:26
  433.3 7.0 copy-start
  433.3 9.4 %copy-start.1 = (bf16[3072,2048]{1,0:T(8,128)(2,1)S(1)}, bf16[3072,2048]{1,0:T(8,128)(2,1)}, u32[]{:S(2)}) copy-start(bf16[3072,2048]{1,0:T(8,128)(2,1)} %all-gather.2.cloned.1.call-done) | copy-start | bytes 37748740
  440.3 3.0 copy-start.5
  755.7 2.2 copy-start.2
  757.9 17.8 %copy-start.7 = (f32[8,120,64]{1,2,0:T(8,128)S(1)}, f32[8,120,64]{1,2,0:T(8,128)}, u32[]{:S(2)}) copy-start(f32[8,120,64]{1,2,0:T(8,128)} %get-tuple-element.6) | copy-start | bytes 737284
Sparse Core Ops, SparseCore 0:
  12.7 282.8 all-reduce.3
  301.9 131.3 all-gather.1
  450.2 302.5 all-reduce.5
where the time goes:
time: 787 us; the launch traced here: 783 us
  waiting for transfers between devices  717 us (91%)
  matrix products  28.5 us (4%)
  blocking collectives  14.3 us (2%)
  between operations  13.9 us (2%)
    psum x1, waiting for transfers between devices, per_device(): merged = lax.psum(partial_rows, 'cells') / total_cells  303 us
    psum x1, waiting for transfers between devices, per_device(): gram = lax.psum(raw_gram, 'cells') / total_cells  283 us
    all_gather x1, waiting for transfers between devices, per_device(): everyone = lax.all_gather(basis, 'runs', axis=0, tiled=True)  131 us
  transfers between devices with their start and end apart: 3, of which 3 were waited for; matrix products, arithmetic and copies ran while one was open for 0% of the time, Pallas kernels for 0%

commit v1 on v0

v1 whole, which is shorter than its diff:
```python
import jax
import jax.numpy as jnp
from jax import lax
from jax.experimental import pallas as pl
from jax.experimental.pallas import tpu as pltpu
from jax.sharding import Mesh
from jax.sharding import PartitionSpec as P

RUNS = ("z_lo", "y")
CELLS = ("x", "z_hi", "core")
F32 = jnp.float32
BF16 = jnp.bfloat16
PARAMS = pltpu.CompilerParams(vmem_limit_bytes=40 << 20)


def send_to(x, da, db):
    pairs = [
        (a * 4 + b, (a + da) % 2 * 4 + (b + db) % 4) for a in range(2) for b in range(4)
    ]
    return lax.ppermute(x, RUNS, pairs)


def swap_cores(x):
    return lax.ppermute(x, "core", [(0, 1), (1, 0)])


def spread(x, axes):
    n = lax.axis_size(axes)
    return lax.all_to_all(jnp.broadcast_to(x[None], (n,) + x.shape), axes, 0, 0, tiled=True)


def rows_times(a, b):
    return lax.dot_general(a, b, (((1,), (1,)), ((), ())), preferred_element_type=F32)


def times_rows(a, b):
    return lax.dot_general(a, b, (((0,), (0,)), ((), ())), preferred_element_type=F32)


def project_kernel(spot, fields, vectors, left, right, far, squares):
    value = times_rows(vectors[0], fields[0])
    squares[0] = jnp.sum(value * value, axis=1, keepdims=True)
    value = value.astype(BF16)
    half = value.shape[1] // 2
    left[...] = value[:, :half]
    right[...] = value[:, half:]
    far[...] = jnp.where(spot[1] // 2 == 0, value[:, half:], value[:, :half])


def project(spot, fields, vectors):
    runs, months, cells = fields.shape
    modes = vectors.shape[2]
    half = pl.BlockSpec((modes, cells // 2), lambda r, spot: (r, 0))
    out = jax.ShapeDtypeStruct((runs * modes, cells // 2), BF16)
    return pl.pallas_call(
        project_kernel,
        grid_spec=pltpu.PrefetchScalarGridSpec(
            num_scalar_prefetch=1,
            grid=(runs,),
            in_specs=[
                pl.BlockSpec((1, months, cells), lambda r, spot: (r, 0, 0)),
                pl.BlockSpec((1, months, modes), lambda r, spot: (r, 0, 0)),
            ],
            out_specs=[half] * 3 + [pl.BlockSpec((1, modes, 1), lambda r, spot: (r, 0, 0))],
        ),
        out_shape=[out] * 3 + [jax.ShapeDtypeStruct((runs, modes, 1), F32)],
        cost_estimate=pl.CostEstimate(
            flops=2 * runs * months * modes * cells,
            bytes_accessed=fields.size * 4,
            transcendentals=0,
        ),
        compiler_params=PARAMS,
    )(spot, fields, vectors)


def gram_kernel(fields, gram):
    months = fields.shape[1]
    gram[0] = jnp.zeros_like(gram[0])
    gram[0, :months, :months] = rows_times(fields[0], fields[0])


def gram_of(fields):
    runs, months, cells = fields.shape
    return pl.pallas_call(
        gram_kernel,
        grid=(runs,),
        in_specs=[pl.BlockSpec((1, months, cells), lambda r: (r, 0, 0))],
        out_specs=pl.BlockSpec((1, 128, 128), lambda r: (r, 0, 0)),
        out_shape=jax.ShapeDtypeStruct((runs, 128, 128), F32),
        cost_estimate=pl.CostEstimate(
            flops=2 * runs * months * months * cells,
            bytes_accessed=fields.size * 2,
            transcendentals=0,
        ),
        compiler_params=PARAMS,
    )(fields)


def pcs_kernel(first, second, mode, norms, out):
    months, common = first.shape[1], mode.shape[0]
    out[0] = jnp.zeros_like(out[0])
    out[0, :months, :common] = rows_times(first[0], mode[...])
    out[0, :months, common:] = rows_times(second[0], mode[...])
    out[0, months : months + 1, :] = norms[...]


def pcs_of(fields, mode, norms):
    runs, months, cells = fields.shape
    return pl.pallas_call(
        pcs_kernel,
        grid=(runs // 2,),
        in_specs=[
            pl.BlockSpec((1, months, cells), lambda r: (r, 0, 0)),
            pl.BlockSpec((1, months, cells), lambda r: (r + 4, 0, 0)),
            pl.BlockSpec(mode.shape, lambda r: (0, 0)),
            pl.BlockSpec(norms.shape, lambda r: (0, 0)),
        ],
        out_specs=pl.BlockSpec((1, 128, 128), lambda r: (r, 0, 0)),
        out_shape=jax.ShapeDtypeStruct((runs // 2, 128, 128), F32),
        cost_estimate=pl.CostEstimate(
            flops=2 * fields.size * mode.shape[0],
            bytes_accessed=fields.size * 2,
            transcendentals=0,
        ),
        compiler_params=PARAMS,
    )(fields, fields, mode, norms)


def put(spot, run, value, keep, send):
    value = value.astype(BF16)
    rows = value.shape[0]
    size = rows // 8

    def store(first, second):
        for x in range(4):
            for k in range(rows // 128):
                at = run * (rows // 128) + k
                columns = slice(k * 128, (k + 1) * 128)
                first[x, at] = value[x * size : (x + 1) * size, columns]
                second[x, at] = value[(x + 4) * size : (x + 5) * size, columns]

    @pl.when(spot[2] == 0)
    def _():
        store(keep, send)

    @pl.when(spot[2] != 0)
    def _():
        store(send, keep)


def put_product(spot, run, swapped, mine, theirs, keep, send):
    @pl.when(swapped == 0)
    def _():
        put(spot, run, rows_times(mine, theirs), keep, send)

    @pl.when(swapped != 0)
    def _():
        put(spot, run, rows_times(theirs, mine), keep, send)


def wrap(x):
    return lax.rem(x + 4, 4)


def chosen(flag, left, right):
    return jnp.where(flag == 0, left[...], right[...])


def blocks_kernel(
    spot, left, right, down, up, over, z_left, z_right, z_down, z_up, z_over, keep, send
):
    a, b = spot[0], spot[1]
    own = rows_times(left[...], left[...]) + rows_times(right[...], right[...])
    put(spot, a * 4 + b, own, keep, send)
    below, above, across = wrap(b + 1), wrap(b - 1), wrap(b + 2)
    middle = chosen(b // 2, left, right)
    beside = chosen(a, z_left, z_right)
    for run, swapped, mine, theirs in (
        (a * 4 + below, (below < b).astype(jnp.int32), left[...], down),
        (a * 4 + above, (above < b).astype(jnp.int32), right[...], up),
        (a * 4 + across, b // 2, middle, over),
        (4 - a * 4 + b, a, chosen(a, left, right), beside),
        (4 - a * 4 + below, a, left[...], z_down),
        (4 - a * 4 + above, a, right[...], z_up),
        (4 - a * 4 + across, a, middle, z_over),
    ):
        put_product(spot, run, swapped, mine, theirs[...], keep, send)


def blocks_of(spot, left, *others):
    rows, cells = left.shape
    out = jax.ShapeDtypeStruct((4, 8 * rows // 128, rows // 8, 128), BF16)
    whole = pl.BlockSpec(memory_space=pltpu.VMEM)
    return pl.pallas_call(
        blocks_kernel,
        in_specs=[pl.BlockSpec(memory_space=pltpu.SMEM)] + [whole] * (1 + len(others)),
        out_specs=[whole, whole],
        out_shape=[out, out],
        cost_estimate=pl.CostEstimate(
            flops=18 * rows * rows * cells, bytes_accessed=24 * left.size, transcendentals=0
        ),
        compiler_params=PARAMS,
    )(spot, left, *others)


def assemble_kernel(spot, own, other, row, col, out):
    j = pl.program_id(0)
    mine = spot[0] * 4 + spot[1]
    rows = out.shape[0]
    size, slabs = rows // 8, rows // 128
    here = pl.ds(pl.multiple_of(lax.rem(j, 2) * size * slabs, 16), size * slabs)
    parts = []
    for core in range(2):
        for x in range(4):
            held = jnp.where(spot[2] == core, own[x, 0, here], other[x, 0, here])
            parts.append(
                jnp.concatenate([held[k * size : (k + 1) * size] for k in range(slabs)], axis=1)
            )
    value = jnp.concatenate(parts, axis=0).astype(F32)

    @pl.when(j >= mine)
    def _():
        out[...] = value * row[...] * col[0]

    @pl.when(j < mine)
    def _():
        out[...] = value.T * row[...] * col[0]


def assemble(spot, own, other, row, col):
    rows = row.shape[0]
    held = pl.BlockSpec((4, 1) + own.shape[2:], lambda j, spot: (0, j // 2, 0, 0))
    return pl.pallas_call(
        assemble_kernel,
        grid_spec=pltpu.PrefetchScalarGridSpec(
            num_scalar_prefetch=1,
            grid=(8,),
            in_specs=[
                held,
                held,
                pl.BlockSpec((rows, 1), lambda j, spot: (0, 0)),
                pl.BlockSpec((1, 1, rows), lambda j, spot: (j, 0, 0)),
            ],
            out_specs=pl.BlockSpec((rows, rows), lambda j, spot: (0, j)),
        ),
        out_shape=jax.ShapeDtypeStruct((rows, 8 * rows), F32),
        compiler_params=PARAMS,
    )(spot, own, other, row, col)


def sum_of(parts):
    return jnp.sum(parts.astype(F32), axis=0)


def split(x):
    high = lax.reduce_precision(x, 8, 7)
    return jnp.concatenate([high.astype(BF16), (x - high).astype(BF16)], axis=0)


def scatter_x(parts):
    return sum_of(lax.all_to_all(parts, "x", 0, 0, tiled=True))


def together(work, *arrays):
    def nothing(*arrays):
        return jax.tree.map(lambda x: jnp.zeros(x.shape, x.dtype), jax.eval_shape(work, *arrays))

    return lax.cond(lax.axis_index("core") < 2, work, nothing, *arrays)


def per_device(fields, vectors, combos):
    runs, months, cells = fields.shape
    modes = vectors.shape[2]
    common = combos.shape[1]
    rows = runs * modes
    total = cells * lax.axis_size(CELLS)
    a, b, core = (lax.axis_index(name) for name in ("z_lo", "y", "core"))
    spot = jnp.stack([a, b, core]).astype(jnp.int32)
    barrier = lax.optimization_barrier

    left, right, far, squares = project(spot, fields, vectors)
    near = (send_to(left, 0, -1), send_to(right, 0, 1), send_to(far, 0, 2))
    z_left, z_right = send_to(left, 1, 0), send_to(right, 1, 0)
    weights = lax.dynamic_slice_in_dim(combos, lax.axis_index(RUNS) * rows, rows, 0)

    def scale_work(squares):
        scale = jnp.sum(spread(squares.reshape(3, rows // 3), CELLS), axis=0)
        return scale.reshape(runs, modes) / total

    def mode_work(fields, vectors, weights, scale):
        projected = jnp.einsum("rmk,rmc->rkc", vectors, fields, preferred_element_type=F32)
        basis = (projected * lax.rsqrt(scale)[:, :, None]).astype(BF16).reshape(rows, cells)
        part = times_rows(weights, basis).reshape(8, common // 8, cells)
        part = jnp.concatenate([part, jnp.broadcast_to(scale[None], (8, runs, modes))], axis=2)
        part = lax.all_to_all(part, RUNS, 0, 0, tiled=True)
        return basis, part, gram_of(fields)

    scale = together(scale_work, squares)
    scale, z_left, z_right, *near = barrier((scale, z_left, z_right, *near))
    z_over = jnp.where(b // 2 == 0, z_right, z_left)
    far = (send_to(z_left, 0, -1), send_to(z_right, 0, 1), send_to(z_over, 0, 2))
    basis, part, gram = together(mode_work, fields, vectors, weights, scale)
    part, *far = barrier((part, *far))

    scales = part[:, :, cells:].reshape(8, rows)
    mode = spread(jnp.sum(part[:, :, :cells], axis=0).astype(BF16), RUNS)
    keep, send = blocks_of(spot, left, right, *near, z_left, z_right, *far)
    blocks = (keep.astype(F32) + swap_cores(send).astype(F32)).astype(BF16)
    gram_keep = jnp.where(core == 0, gram[:4], gram[4:])
    gram_send = jnp.where(core == 0, gram[4:], gram[:4])
    gram = (gram_keep + swap_cores(gram_send)).astype(BF16)
    mode = mode.reshape(common, cells)
    mode_wide = mode.astype(F32)
    norms = jnp.sum(mode_wide * mode_wide, axis=1) / total
    norms = jnp.concatenate([norms, norms])[None]
    pcs = pcs_of(fields, mode, norms)
    pcs_keep = jnp.where(core == 0, pcs[:2], pcs[2:])
    pcs_send = jnp.where(core == 0, pcs[2:], pcs[:2])
    pcs = split(pcs_keep + swap_cores(pcs_send))
    extra = jnp.concatenate([gram, pcs], axis=0)
    extra = extra.reshape(8, 4, 32, 128).transpose(1, 0, 2, 3).reshape(4, 256, 128)

    half = rows * 3
    blocks = scatter_x(jnp.concatenate([blocks.reshape(4, half, 128), extra], axis=1))
    extra, blocks = blocks[half:], blocks[:half].astype(BF16).reshape(8, half // 8, 128)
    others = lax.all_to_all(blocks, RUNS, 0, 0, tiled=True)
    same = lax.broadcasted_iota(jnp.int32, (8, 1, 1), 0) == a * 4 + b
    others = jnp.where(same, 0.0, others.astype(F32))
    blocks = (blocks.astype(F32) + others).astype(BF16).reshape(4, half // 4, 128)
    pcs = split(extra[128:192] + extra[192:]).reshape(2, 4, 16, 128)
    pieces = [blocks, extra[:128].astype(BF16).reshape(4, 32, 128), pcs[0], pcs[1]]
    pieces = jnp.concatenate(pieces, axis=1)
    pieces = sum_of(lax.all_to_all(pieces, "z_hi", 0, 0, tiled=True))
    pcs = split(pieces[-32:-16] + pieces[-16:])
    pieces = jnp.concatenate([pieces[:-32].astype(BF16), pcs], axis=0)
    own = spread(spread(pieces, "z_hi"), "x")
    other = swap_cores(own)
    row = lax.rsqrt(scale).reshape(rows, 1) / total
    col = lax.rsqrt(scales).reshape(8, 1, rows)
    merged = assemble(spot, own, other, row, col)

    def whole(pieces):
        extra = pieces[:, :, -64:].astype(F32)
        gram = extra[:, :, :32].transpose(1, 0, 2, 3).reshape(4, 128, 128)
        pcs = extra[:, :, 32:48] + extra[:, :, 48:]
        pcs = pcs.reshape(4, 2, 2, 16, 128).transpose(1, 0, 2, 3, 4).reshape(2, 128, 128)
        return gram, pcs

    both = [whole(own), whole(other)]
    gram, pcs = (
        jnp.where(
            core == 0,
            jnp.concatenate([both[0][n], both[1][n]]),
            jnp.concatenate([both[1][n], both[0][n]]),
        )
        for n in range(2)
    )
    gram = gram[:, :months, :months] / total
    inverse = lax.rsqrt(pcs[0, months])
    pcs = pcs[:, :months] * inverse / total
    pcs = jnp.concatenate([pcs[:, :, :common], pcs[:, :, common:]], axis=0)
    eofs = (mode_wide * inverse[:common, None]).astype(BF16)
    return (gram, basis, merged, eofs, pcs)


def solution(mesh):
    fine = Mesh(mesh.devices.reshape(2, 4, 4, 4, 2), RUNS + CELLS)
    return jax.shard_map(
        per_device,
        mesh=fine,
        in_specs=(P(RUNS, None, CELLS), P(RUNS, None, None), P()),
        out_specs=(
            P(RUNS, None, None),
            P(RUNS, CELLS),
            P(RUNS, None),
            P(None, CELLS),
            P(RUNS, None, None),
        ),
        check_vma=False,
    )
```

time: 787 us -> 226 us (0.29)
  waiting for transfers between devices: 717 us -> 28.6 us
  blocking collectives: 14.3 us -> 103 us
  Pallas kernels: 0 us -> 32.9 us
  starting transfers between devices: 0.12 us -> 32.7 us
  matrix products: 28.5 us -> 6.01 us
  between operations: 13.9 us -> 0.99 us
    psum x2 -> x0, waiting for transfers between devices: 586 us -> none  [the longest x1 303 us: per_device(): merged = lax.psum(partial_rows, 'cells') / total_cells]
    all_gather x1 -> x0, waiting for transfers between devices: 131 us -> none  [per_device(): everyone = lax.all_gather(basis, 'runs', axis=0, tiled=True)]
    all_to_all x0 -> x5, blocking collectives: none -> 103 us  [the longest x3 70.3 us: spread(): lax.all_to_all(jnp.broadcast_to(x[None], (n,) + x.shape), axes, 0, 0, til...]
    pallas_call x0 -> x5, Pallas kernels: none -> 32.9 us  [the longest x1 9.86 us: blocks_of(): pl.pallas_call(blocks_kernel, in_specs=[pl.BlockSpec(memory_space=pltpu.S...]
    all_to_all x0 -> x3, waiting for transfers between devices: none -> 27.6 us  [the longest x1 21.4 us: mode_work(): part = lax.all_to_all(part, RUNS, 0, 0, tiled=True)]
    dot_general x7 -> x2, matrix products: 28.5 us -> 6.01 us  [the longest x1 4.2 us: mode_work(): jnp.einsum('rmk,rmc->rkc', vectors, fields, preferred_element_type=F32)]
    ppermute x0 -> x12, starting transfers between devices: none -> 19.7 us  [the longest x8 11.6 us: send_to(): return lax.ppermute(x, RUNS, pairs)]
    psum x1 -> x0, blocking collectives: 14.3 us -> none  [per_device(): norms = lax.psum(local_norms, 'runs')]
  transfers between devices with their start and end apart: 3 -> 15, of which waited for: 3 -> 3; matrix products, arithmetic and copies ran while one was open for 0% -> 6% of each run, Pallas kernels for 0% -> 9%
where the time goes in v1:
time: 226 us; the launch traced here: 225 us
  blocking collectives  103 us (46%)
  Pallas kernels  32.9 us (15%)
  starting transfers between devices  32.7 us (14%)
  waiting for transfers between devices  28.6 us (13%)
  other arithmetic  10.2 us (5%)
  local copies, waits for them, and re-layouts  10.1 us (4%)
  matrix products  6.01 us (3%)
    all_to_all x3, blocking collectives, spread(): lax.all_to_all(jnp.broadcast_to(x[None], (n,) + x.shape), axes, 0, 0, til...  70.3 us
    all_to_all x1, blocking collectives, scatter_x(): return sum_of(lax.all_to_all(parts, 'x', 0, 0, tiled=True))  21.6 us
    all_to_all x1, waiting for transfers between devices, mode_work(): part = lax.all_to_all(part, RUNS, 0, 0, tiled=True)  21.4 us
    ppermute x8, starting transfers between devices, send_to(): return lax.ppermute(x, RUNS, pairs)  11.6 us
    all_to_all x1, blocking collectives, per_device(): pieces = sum_of(lax.all_to_all(pieces, 'z_hi', 0, 0, tiled=True))  11.4 us
    pallas_call x1, Pallas kernels, blocks_of(): pl.pallas_call(blocks_kernel, in_specs=[pl.BlockSpec(memory_space=pltpu.S...  9.86 us
    ppermute x4, starting transfers between devices, swap_cores(): return lax.ppermute(x, 'core', [(0, 1), (1, 0)])  8.2 us
    pallas_call x1, Pallas kernels, project(): pl.pallas_call(project_kernel, grid_spec=pltpu.PrefetchScalarGridSpec(num...  7.33 us
  transfers between devices with their start and end apart: 15, of which 3 were waited for; matrix products, arithmetic and copies ran while one was open for 6% of the time, Pallas kernels for 9%

profile of v1, /device:TPU:1, one launch (start us, length us, event | category | flops | bytes accessed | tf_op | source)
XLA Modules:
  0.0 224.8 jit_solution(611890510098317253)
XLA Ops:
  0.6 1.1 copy.51.vectors
  1.8 7.3 %shard_map.75 = (bf16[384,1024]{1,0:T(8,128)(2,1)S(1)}, bf16[384,1024]{1,0:T(8,128)(2,1)}, bf16[384,1024]{1,0:T(8,128)(2,1)}, f32[8,48,1]{2,1,0:T(8,128)S(1)}) custom-call(s32[3]{0:T(128)S(1)} %pad_add_fusion.spot, bf16[8,120,2048]{2,1,0:T(8,128)(2,1)} %second.1, bf16[8,120,48]{2,1,0:T(8,128)(2,1)S(1)} %copy.51.vectors), custom_call_target="tpu_custom_call" | custom-call | flops 188743680 | bytes 7864320 | tf_op jit(solution)/shard_map/pallas_call | solution.py:55
  9.1 2.5 %collective-permute-start = (bf16[384,1024]{1,0:T(8,128)(2,1)S(1)}, bf16[384,1024]{1,0:T(8,128)(2,1)S(1)}, u32[]{:S(2)}, u32[]{:S(2)}) collective-permute-start(bf16[384,1024]{1,0:T(8,128)(2,1)S(1)} %get-tuple-element.43.left), channel_id=1, source_target_pairs={{0,128},{32,160},{64,192},{96,224},{128,0},{160,32},{192,64},{224,... | collective-permute-start | bytes 2359304 | tf_op jit(solution)/shard_map/ppermute | solution.py:20
  11.6 2.7 %collective-permute-start.2 = (bf16[384,1024]{1,0:T(8,128)(2,1)S(1)}, bf16[384,1024]{1,0:T(8,128)(2,1)}, u32[]{:S(2)}, u32[]{:S(2)}) collective-permute-start(bf16[384,1024]{1,0:T(8,128)(2,1)S(1)} %get-tuple-element.43.left), channel_id=1, source_target_pairs={{0,96},{32,0},{64,32},{96,64},{128,224},{160,128},{192,160},{224,1... | collective-permute-start | bytes 2359304 | tf_op jit(solution)/shard_map/ppermute | solution.py:20
  14.5 1.6 collective-permute-start.4
  16.1 40.1 %conditional.2 = (f32[8,48]{1,0:T(8,128)S(1)}) conditional(s32[]{:T(128)} %convert_element_type.77, () %tuple.26, f32[8,48,1]{2,1,0:T(8,128)S(1)} %get-tuple-element.45), branch_computations={%region_0.0_spmd, %region_1.0_spmd} | conditional | flops 12288 | bytes 211984 | solution.py:268
  16.3 39.7 %all_to_all.38 = f32[32,3,128]{2,1,0:T(4,128)S(1)} all-to-all(f32[32,3,128]{2,1,0:T(4,128)S(1)} %broadcast_in_dim.22), channel_id=1, replica_groups=mesh['z_lo'=2,'y'=4,'x'=4,'z_hi'=4,'core'=2] {'x','z_hi','core'}, dimensions={0} | all-to-all | bytes 98304 | tf_op jit(solution)/shard_map/cond/branch_1_fun/all_to_all | solution.py:29
  56.2 2.8 %collective-permute-start.5 = (bf16[384,1024]{1,0:T(8,128)(2,1)S(1)}, bf16[384,1024]{1,0:T(8,128)(2,1)}, u32[]{:S(2)}, u32[]{:S(2)}) collective-permute-start(bf16[384,1024]{1,0:T(8,128)(2,1)S(1)} %collective-permute-done.z_left), channel_id=1, source_target_pairs={{0,96},{32,0},{64,32},{96,64},{128,224},{160,128},{192,160},{224,1... | collective-permute-start | bytes 2359304 | tf_op jit(solution)/shard_map/ppermute | solution.py:20
  59.2 1.7 collective-permute-start.7
  60.9 40.7 %conditional.3 = (bf16[384,2048]{1,0:T(8,128)(2,1)}, f32[8,8,2096]{2,1,0:T(8,128)}, f32[8,128,128]{2,1,0:T(8,128)}, f32[4,128,128]{2,1,0:T(8,128)S(1)}, f32[4,128,128]{2,1,0:T(8,128)S(1)}) conditional(s32[]{:T(128)} %convert_element_type.77, () %tuple.28, (bf16[8,120,48]{1,2,0:T(8,128)(2,1)}, bf16[8,120,2048]{2,1,0:T(8,128)(2,1)}, ...), branch_computations={%region_3.4_spmd, %region_4.5_spmd} | conditional | flops 762973184 | bytes 16302190 | solution.py:268
  60.9 0.4 copy.53
  61.3 4.2 %multiply_convert_fusion = bf16[8,48,2048]{2,1,0:T(8,128)(2,1)} fusion(bf16[8,120,48]{1,2,0:T(8,128)(2,1)} %get-tuple-element.14, bf16[8,120,2048]{2,1,0:T(8,128)(2,1)} %get-tuple-element.15.fields, f32[8,48]{1,0:T(8,128)S(1)} %rsqrt.19), kind=kOutput, calls=%fused_computation | convolution fusion | flops 190316544 | bytes 5598720 | tf_op jit(solution)/shard_map/cond/branch_1_fun/rmk,rmc->rkc/dot_general | solution.py:291
  65.5 1.8 convolution_bitcast_fusion
  67.3 0.9 pad_maximum_fusion
  68.2 4.2 %all-to-all-start.1 = ((f32[8,8,2096]{2,1,0:T(8,128)}), f32[8,8,2096]{2,1,0:T(8,128)}, u32[]{:S(2)}, u32[]{:S(2)}) async-start(f32[8,8,2096]{2,1,0:T(8,128)} %pad_maximum_fusion), calls=%async_computation.1 | async-start | bytes 1114112 | tf_op jit(solution)/shard_map/cond/branch_1_fun/all_to_all | solution.py:295
  72.4 6.8 %branch_1_fun.1 = f32[8,128,128]{2,1,0:T(8,128)} custom-call(bf16[8,120,2048]{2,1,0:T(8,128)(2,1)} %get-tuple-element.15.fields), custom_call_target="tpu_custom_call" | custom-call | flops 471859200 | bytes 3932160 | tf_op jit(solution)/shard_map/cond/branch_1_fun/pallas_call | solution.py:84
  79.1 1.1 fusion.9
  80.2 21.4 %all-to-all-done.1 = f32[8,8,2096]{2,1,0:T(8,128)} async-done(((f32[8,8,2096]{2,1,0:T(8,128)}), f32[8,8,2096]{2,1,0:T(8,128)}, u32[]{:S(2)}, u32[]{:S(2)}) %all-to-all-start.1) | async-done | bytes 536608 | tf_op jit(solution)/shard_map/cond/branch_1_fun/all_to_all | solution.py:295
  101.6 1.1 slice_reduce_fusion
  102.7 0.7 broadcast_in_dim.34
  103.4 3.4 %all-to-all-start.2 = ((bf16[8,8,2048]{2,1,0:T(8,128)(2,1)}), bf16[8,8,2048]{2,1,0:T(8,128)(2,1)S(1)}, u32[]{:S(2)}, u32[]{:S(2)}) async-start(bf16[8,8,2048]{2,1,0:T(8,128)(2,1)} %broadcast_in_dim.34), calls=%async_computation.2 | async-start | bytes 524288 | tf_op jit(solution)/shard_map/all_to_all | solution.py:29
  106.8 0.7 broadcast_select_fusion.1
  107.6 1.5 collective-permute-start.9
  109.1 1.1 copy-done.1
  110.3 9.9 %shard_map.76 = (bf16[4,24,48,128]{3,2,1,0:T(8,128)(2,1)S(1)}, bf16[4,24,48,128]{3,2,1,0:T(8,128)(2,1)}) custom-call(s32[3]{0:T(128)S(1)} %pad_add_fusion.spot, bf16[384,1024]{1,0:T(8,128)(2,1)S(1)} %copy-done.1, bf16[384,1024]{1,0:T(8,128)(2,1)} %get-tuple-element.44.right, bf16[384,1024]{1,0:T(8,128)(2,1)} %collective-permute-done.2.down, ...), custom_call_target="tpu_custom_call" | custom-call | flops 2717908992 | bytes 9437184 | tf_op jit(solution)/shard_map/pallas_call | solution.py:194
  120.4 3.9 %shard_map.77 = f32[4,128,128]{2,1,0:T(8,128)S(1)} custom-call(bf16[8,120,2048]{2,1,0:T(8,128)(2,1)} %second.1, bf16[8,120,2048]{2,1,0:T(8,128)(2,1)} %second.1, bf16[64,2048]{1,0:T(8,128)(2,1)S(1)} %bitcast.41, f32[1,128]{1,0:T(1,128)S(1)} %maximum_bitcast_fusion.norms), custom_call_target="tpu_custom_call" | custom-call | flops 251658240 | bytes 3932160 | tf_op jit(solution)/shard_map/pallas_call | solution.py:109
  124.4 0.6 collective-permute-start.10
  125.0 1.0 add_convert_fusion.2
  126.2 0.3 add_convert_fusion
  126.6 21.6 %all_to_all.39 = bf16[4,1408,128]{2,1,0:T(8,128)(2,1)S(1)} all-to-all(bf16[4,1408,128]{2,1,0:T(8,128)(2,1)S(1)} %pad_maximum_fusion.1), channel_id=1, replica_groups=mesh['z_lo'=2,'y'=4,'x'=4,'z_hi'=4,'core'=2] {'x'}, dimensions={0} | all-to-all | bytes 2883584 | tf_op jit(solution)/shard_map/all_to_all | solution.py:261
  148.1 0.2 convert_reduce_fusion
  148.4 0.7 slice.135
  149.1 5.3 %all-to-all-start.4 = ((bf16[8,144,128]{2,1,0:T(8,128)(2,1)}), bf16[8,144,128]{2,1,0:T(8,128)(2,1)S(1)}, u32[]{:S(2)}, u32[]{:S(2)}) async-start(bf16[8,144,128]{2,1,0:T(8,128)(2,1)} %bitcast.11), calls=%async_computation.4 | async-start | bytes 589824 | tf_op jit(solution)/shard_map/all_to_all | solution.py:326
  154.5 6.2 %all-to-all-done.4 = bf16[8,144,128]{2,1,0:T(8,128)(2,1)S(1)} async-done(((bf16[8,144,128]{2,1,0:T(8,128)(2,1)}), bf16[8,144,128]{2,1,0:T(8,128)(2,1)S(1)}, u32[]{:S(2)}, u32[]{:S(2)}) %all-to-all-start.4) | async-done | bytes 294944 | tf_op jit(solution)/shard_map/all_to_all | solution.py:326
  160.7 1.1 add_convert_fusion.1
  161.9 11.4 %all_to_all.40 = bf16[4,352,128]{2,1,0:T(8,128)(2,1)S(1)} all-to-all(bf16[4,352,128]{2,1,0:T(8,128)(2,1)S(1)} %pad_maximum_fusion.5), channel_id=1, replica_groups=mesh['z_lo'=2,'y'=4,'x'=4,'z_hi'=4,'core'=2] {'z_hi'}, dimensions={0} | all-to-all | bytes 720896 | tf_op jit(solution)/shard_map/all_to_all | solution.py:333
  173.4 13.9 %all_to_all.41 = bf16[4,352,128]{2,1,0:T(8,128)(2,1)S(1)} all-to-all(bf16[4,352,128]{2,1,0:T(8,128)(2,1)S(1)} %broadcast_in_dim.38), channel_id=1, replica_groups=mesh['z_lo'=2,'y'=4,'x'=4,'z_hi'=4,'core'=2] {'z_hi'}, dimensions={0} | all-to-all | bytes 720896 | tf_op jit(solution)/shard_map/all_to_all | solution.py:29
  187.5 16.7 %all_to_all.42.own = bf16[4,4,352,128]{3,2,1,0:T(8,128)(2,1)S(1)} all-to-all(bf16[4,4,352,128]{3,2,1,0:T(8,128)(2,1)S(1)} %broadcast_in_dim.54), channel_id=1, replica_groups=mesh['z_lo'=2,'y'=4,'x'=4,'z_hi'=4,'core'=2] {'x'}, dimensions={0} | all-to-all | bytes 2883584 | tf_op jit(solution)/shard_map/all_to_all | solution.py:29
  204.1 6.1 %collective-permute-start.11 = (bf16[4,4,352,128]{3,2,1,0:T(8,128)(2,1)S(1)}, bf16[4,4,352,128]{3,2,1,0:T(8,128)(2,1)S(1)}, u32[]{:S(2)}, u32[]{:S(2)}) collective-permute-start(bf16[4,4,352,128]{3,2,1,0:T(8,128)(2,1)S(1)} %all_to_all.42.own), channel_id=1, source_target_pairs={{0,1},{1,0},{2,3},{3,2},{4,5},{5,4},{6,7},{7,6},{8,9},{9,8},{10,11... | collective-permute-start | bytes 4325384 | tf_op jit(solution)/shard_map/ppermute | solution.py:24
  210.3 0.8 slice_rsqrt_fusion
  211.3 0.7 copy.55
  212.0 1.0 collective-permute-done.11.other
  213.1 0.7 copy.56
  214.1 0.8 pad_maximum_fusion.4
  214.9 1.9 copy.60
  216.8 2.1 fusion.3
  218.9 0.8 multiply_convert_fusion.1
  219.8 5.1 %shard_map.78 = f32[384,3072]{1,0:T(8,128)} custom-call(s32[3]{0:T(128)S(1)} %pad_add_fusion.spot, bf16[4,4,352,128]{3,2,1,0:T(8,128)(2,1)S(1)} %all_to_all.42.own, bf16[4,4,352,128]{3,2,1,0:T(8,128)(2,1)S(1)} %collective-permute-done.11.other, f32[384,1]{1,0:T(8,128)S(1)} %div.54.row, f32[8,1,384]{2,1,0:T(1,128)S(1)} %rsqrt.26.col), custom_call_target="tpu_custom_call" | custom-call | tf_op jit(solution)/shard_map/pallas_call | solution.py:233
  (68 shorter events, 2.1 us)
Async XLA Ops:
  9.1 51.8 %copy-start = (bf16[384,1024]{1,0:T(8,128)(2,1)}, bf16[384,1024]{1,0:T(8,128)(2,1)S(1)}, u32[]{:S(2)}) copy-start(bf16[384,1024]{1,0:T(8,128)(2,1)S(1)} %get-tuple-element.43.left) | copy-start | bytes 2359300
  9.1 51.8 %copy-start.2 = (bf16[3072,64]{0,1:T(8,128)(2,1)S(1)}, bf16[3072,64]{0,1:T(8,128)(2,1)}, u32[]{:S(2)}) copy-start(bf16[3072,64]{0,1:T(8,128)(2,1)} %param.9) | copy-start | bytes 1179652
  9.1 47.1 %collective-permute-start = (bf16[384,1024]{1,0:T(8,128)(2,1)S(1)}, bf16[384,1024]{1,0:T(8,128)(2,1)S(1)}, u32[]{:S(2)}, u32[]{:S(2)}) collective-permute-start(bf16[384,1024]{1,0:T(8,128)(2,1)S(1)} %get-tuple-element.43.left), channel_id=1, source_target_pairs={{0,128},{32,160},{64,192},{96,224},{128,0},{160,32},{192,64},{224,... | collective-permute-start | bytes 2359304 | tf_op jit(solution)/shard_map/ppermute | solution.py:20
  11.6 44.6 %collective-permute-start.2 = (bf16[384,1024]{1,0:T(8,128)(2,1)S(1)}, bf16[384,1024]{1,0:T(8,128)(2,1)}, u32[]{:S(2)}, u32[]{:S(2)}) collective-permute-start(bf16[384,1024]{1,0:T(8,128)(2,1)S(1)} %get-tuple-element.43.left), channel_id=1, source_target_pairs={{0,96},{32,0},{64,32},{96,64},{128,224},{160,128},{192,160},{224,1... | collective-permute-start | bytes 2359304 | tf_op jit(solution)/shard_map/ppermute | solution.py:20
  14.4 41.8 %collective-permute-start.1 = (bf16[384,1024]{1,0:T(8,128)(2,1)}, bf16[384,1024]{1,0:T(8,128)(2,1)S(1)}, u32[]{:S(2)}, u32[]{:S(2)}) collective-permute-start(bf16[384,1024]{1,0:T(8,128)(2,1)} %get-tuple-element.44.right), channel_id=1, source_target_pairs={{0,128},{32,160},{64,192},{96,224},{128,0},{160,32},{192,64},{224,... | collective-permute-start | bytes 2359304 | tf_op jit(solution)/shard_map/ppermute | solution.py:20
  14.5 41.8 %collective-permute-start.3 = (bf16[384,1024]{1,0:T(8,128)(2,1)}, bf16[384,1024]{1,0:T(8,128)(2,1)}, u32[]{:S(2)}, u32[]{:S(2)}) collective-permute-start(bf16[384,1024]{1,0:T(8,128)(2,1)} %get-tuple-element.44.right), channel_id=1, source_target_pairs={{0,32},{32,64},{64,96},{96,0},{128,160},{160,192},{192,224},{224,1... | collective-permute-start | bytes 2359304 | tf_op jit(solution)/shard_map/ppermute | solution.py:20
  14.5 41.8 %collective-permute-start.4 = (bf16[384,1024]{1,0:T(8,128)(2,1)}, bf16[384,1024]{1,0:T(8,128)(2,1)}, u32[]{:S(2)}, u32[]{:S(2)}) collective-permute-start(bf16[384,1024]{1,0:T(8,128)(2,1)} %get-tuple-element.46), channel_id=1, source_target_pairs={{0,64},{32,96},{64,0},{96,32},{128,192},{160,224},{192,128},{224,1... | collective-permute-start | bytes 2359304 | tf_op jit(solution)/shard_map/ppermute | solution.py:20
  56.2 45.4 %collective-permute-start.5 = (bf16[384,1024]{1,0:T(8,128)(2,1)S(1)}, bf16[384,1024]{1,0:T(8,128)(2,1)}, u32[]{:S(2)}, u32[]{:S(2)}) collective-permute-start(bf16[384,1024]{1,0:T(8,128)(2,1)S(1)} %collective-permute-done.z_left), channel_id=1, source_target_pairs={{0,96},{32,0},{64,32},{96,64},{128,224},{160,128},{192,160},{224,1... | collective-permute-start | bytes 2359304 | tf_op jit(solution)/shard_map/ppermute | solution.py:20
  59.1 42.6 %collective-permute-start.6 = (bf16[384,1024]{1,0:T(8,128)(2,1)S(1)}, bf16[384,1024]{1,0:T(8,128)(2,1)}, u32[]{:S(2)}, u32[]{:S(2)}) collective-permute-start(bf16[384,1024]{1,0:T(8,128)(2,1)S(1)} %collective-permute-done.1.z_right), channel_id=1, source_target_pairs={{0,32},{32,64},{64,96},{96,0},{128,160},{160,192},{192,224},{224,1... | collective-permute-start | bytes 2359304 | tf_op jit(solution)/shard_map/ppermute | solution.py:20
  59.2 42.5 %collective-permute-start.7 = (bf16[384,1024]{1,0:T(8,128)(2,1)S(1)}, bf16[384,1024]{1,0:T(8,128)(2,1)}, u32[]{:S(2)}, u32[]{:S(2)}) collective-permute-start(bf16[384,1024]{1,0:T(8,128)(2,1)S(1)} %broadcast_select_fusion), channel_id=1, source_target_pairs={{0,64},{32,96},{64,0},{96,32},{128,192},{160,224},{192,128},{224,1... | collective-permute-start | bytes 2359304 | tf_op jit(solution)/shard_map/ppermute | solution.py:20
  68.2 33.4 %all-to-all-start.1 = ((f32[8,8,2096]{2,1,0:T(8,128)}), f32[8,8,2096]{2,1,0:T(8,128)}, u32[]{:S(2)}, u32[]{:S(2)}) async-start(f32[8,8,2096]{2,1,0:T(8,128)} %pad_maximum_fusion), calls=%async_computation.1 | async-start | bytes 1114112 | tf_op jit(solution)/shard_map/cond/branch_1_fun/all_to_all | solution.py:295
  103.4 16.7 %all-to-all-start.2 = ((bf16[8,8,2048]{2,1,0:T(8,128)(2,1)}), bf16[8,8,2048]{2,1,0:T(8,128)(2,1)S(1)}, u32[]{:S(2)}, u32[]{:S(2)}) async-start(bf16[8,8,2048]{2,1,0:T(8,128)(2,1)} %broadcast_in_dim.34), calls=%async_computation.2 | async-start | bytes 524288 | tf_op jit(solution)/shard_map/all_to_all | solution.py:29
  107.6 17.4 %collective-permute-start.9 = (f32[4,128,128]{2,1,0:T(8,128)}, f32[4,128,128]{2,1,0:T(8,128)}, u32[]{:S(2)}, u32[]{:S(2)}) collective-permute-start(f32[4,128,128]{2,1,0:T(8,128)} %broadcast_select_fusion.1), channel_id=1, source_target_pairs={{0,1},{1,0},{2,3},{3,2},{4,5},{5,4},{6,7},{7,6},{8,9},{9,8},{10,11... | collective-permute-start | bytes 786440 | tf_op jit(solution)/shard_map/ppermute | solution.py:24
  109.1 1.1 copy-start.1
  120.1 6.0 %collective-permute-start.8 = (bf16[4,24,48,128]{3,2,1,0:T(8,128)(2,1)}, bf16[4,24,48,128]{3,2,1,0:T(8,128)(2,1)S(1)}, u32[]{:S(2)}, u32[]{:S(2)}) collective-permute-start(bf16[4,24,48,128]{3,2,1,0:T(8,128)(2,1)} %get-tuple-element.58), channel_id=1, source_target_pairs={{0,1},{1,0},{2,3},{3,2},{4,5},{5,4},{6,7},{7,6},{8,9},{9,8},{10,11... | collective-permute-start | bytes 3538952 | tf_op jit(solution)/shard_map/ppermute | solution.py:24
  124.4 1.6 collective-permute-start.10
  149.1 11.6 %all-to-all-start.4 = ((bf16[8,144,128]{2,1,0:T(8,128)(2,1)}), bf16[8,144,128]{2,1,0:T(8,128)(2,1)S(1)}, u32[]{:S(2)}, u32[]{:S(2)}) async-start(bf16[8,144,128]{2,1,0:T(8,128)(2,1)} %bitcast.11), calls=%async_computation.4 | async-start | bytes 589824 | tf_op jit(solution)/shard_map/all_to_all | solution.py:326
  204.1 8.9 %collective-permute-start.11 = (bf16[4,4,352,128]{3,2,1,0:T(8,128)(2,1)S(1)}, bf16[4,4,352,128]{3,2,1,0:T(8,128)(2,1)S(1)}, u32[]{:S(2)}, u32[]{:S(2)}) collective-permute-start(bf16[4,4,352,128]{3,2,1,0:T(8,128)(2,1)S(1)} %all_to_all.42.own), channel_id=1, source_target_pairs={{0,1},{1,0},{2,3},{3,2},{4,5},{5,4},{6,7},{7,6},{8,9},{9,8},{10,11... | collective-permute-start | bytes 4325384 | tf_op jit(solution)/shard_map/ppermute | solution.py:24

commit v2 on v1

--- a/solution.py
+++ b/solution.py
@@ -96,15 +96,18 @@
     )(fields)
 
 
-def pcs_kernel(first, second, mode, norms, out):
+def pcs_kernel(first, second, mode, out):
     months, common = first.shape[1], mode.shape[0]
+    wide = mode[...].astype(F32)
+    norms = jnp.sum(wide * wide, axis=1, keepdims=True)
     out[0] = jnp.zeros_like(out[0])
-    out[0, :months, :common] = rows_times(first[0], mode[...])
-    out[0, :months, common:] = rows_times(second[0], mode[...])
-    out[0, months : months + 1, :] = norms[...]
-
-
-def pcs_of(fields, mode, norms):
+    out[0, :common, :months] = rows_times(mode[...], first[0])
+    out[0, common:, :months] = rows_times(mode[...], second[0])
+    out[0, :common, months : months + 1] = norms
+    out[0, common:, months : months + 1] = norms
+
+
+def pcs_of(fields, mode):
     runs, months, cells = fields.shape
     return pl.pallas_call(
         pcs_kernel,
@@ -113,7 +116,6 @@
             pl.BlockSpec((1, months, cells), lambda r: (r, 0, 0)),
             pl.BlockSpec((1, months, cells), lambda r: (r + 4, 0, 0)),
             pl.BlockSpec(mode.shape, lambda r: (0, 0)),
-            pl.BlockSpec(norms.shape, lambda r: (0, 0)),
         ],
         out_specs=pl.BlockSpec((1, 128, 128), lambda r: (r, 0, 0)),
         out_shape=jax.ShapeDtypeStruct((runs // 2, 128, 128), F32),
@@ -123,7 +125,7 @@
             transcendentals=0,
         ),
         compiler_params=PARAMS,
-    )(fields, fields, mode, norms)
+    )(fields, fields, mode)
 
 
 def put(spot, run, value, keep, send):
@@ -166,38 +168,44 @@
     return jnp.where(flag == 0, left[...], right[...])
 
 
-def blocks_kernel(
-    spot, left, right, down, up, over, z_left, z_right, z_down, z_up, z_over, keep, send
-):
-    a, b = spot[0], spot[1]
+def near_kernel(spot, left, right, down, up, over, keep, send):
+    b = spot[1]
     own = rows_times(left[...], left[...]) + rows_times(right[...], right[...])
-    put(spot, a * 4 + b, own, keep, send)
+    put(spot, b, own, keep, send)
     below, above, across = wrap(b + 1), wrap(b - 1), wrap(b + 2)
     middle = chosen(b // 2, left, right)
-    beside = chosen(a, z_left, z_right)
     for run, swapped, mine, theirs in (
-        (a * 4 + below, (below < b).astype(jnp.int32), left[...], down),
-        (a * 4 + above, (above < b).astype(jnp.int32), right[...], up),
-        (a * 4 + across, b // 2, middle, over),
-        (4 - a * 4 + b, a, chosen(a, left, right), beside),
-        (4 - a * 4 + below, a, left[...], z_down),
-        (4 - a * 4 + above, a, right[...], z_up),
-        (4 - a * 4 + across, a, middle, z_over),
+        (below, (below < b).astype(jnp.int32), left[...], down),
+        (above, (above < b).astype(jnp.int32), right[...], up),
+        (across, b // 2, middle, over),
     ):
         put_product(spot, run, swapped, mine, theirs[...], keep, send)
 
 
-def blocks_of(spot, left, *others):
+def far_kernel(spot, left, right, z_left, z_right, down, up, over, keep, send):
+    a, b = spot[0], spot[1]
+    beside = chosen(a, z_left, z_right)
+    middle = chosen(b // 2, left, right)
+    for run, mine, theirs in (
+        (b, chosen(a, left, right), beside),
+        (wrap(b + 1), left[...], down[...]),
+        (wrap(b - 1), right[...], up[...]),
+        (wrap(b + 2), middle, over[...]),
+    ):
+        put_product(spot, run, a, mine, theirs, keep, send)
+
+
+def blocks_of(kernel, spot, left, *others):
     rows, cells = left.shape
-    out = jax.ShapeDtypeStruct((4, 8 * rows // 128, rows // 8, 128), BF16)
+    out = jax.ShapeDtypeStruct((4, 4 * rows // 128, rows // 8, 128), BF16)
     whole = pl.BlockSpec(memory_space=pltpu.VMEM)
     return pl.pallas_call(
-        blocks_kernel,
+        kernel,
         in_specs=[pl.BlockSpec(memory_space=pltpu.SMEM)] + [whole] * (1 + len(others)),
         out_specs=[whole, whole],
         out_shape=[out, out],
         cost_estimate=pl.CostEstimate(
-            flops=18 * rows * rows * cells, bytes_accessed=24 * left.size, transcendentals=0
+            flops=9 * rows * rows * cells, bytes_accessed=12 * left.size, transcendentals=0
         ),
         compiler_params=PARAMS,
     )(spot, left, *others)
@@ -287,46 +295,52 @@
         scale = jnp.sum(spread(squares.reshape(3, rows // 3), CELLS), axis=0)
         return scale.reshape(runs, modes) / total
 
-    def mode_work(fields, vectors, weights, scale):
+    def mode_work(fields, vectors, weights, scale, left, right, *near):
+        keep, send = blocks_of(near_kernel, spot, left, right, *near)
+        blocks = (keep.astype(F32) + swap_cores(send).astype(F32)).astype(BF16)
+        blocks = scatter_x(blocks.reshape(4, rows * 3 // 2, 128)).astype(BF16)
         projected = jnp.einsum("rmk,rmc->rkc", vectors, fields, preferred_element_type=F32)
         basis = (projected * lax.rsqrt(scale)[:, :, None]).astype(BF16).reshape(rows, cells)
         part = times_rows(weights, basis).reshape(8, common // 8, cells)
         part = jnp.concatenate([part, jnp.broadcast_to(scale[None], (8, runs, modes))], axis=2)
+        part, blocks = barrier((part, blocks))
         part = lax.all_to_all(part, RUNS, 0, 0, tiled=True)
-        return basis, part, gram_of(fields)
+        return basis, part, gram_of(fields), blocks
 
     scale = together(scale_work, squares)
     scale, z_left, z_right, *near = barrier((scale, z_left, z_right, *near))
     z_over = jnp.where(b // 2 == 0, z_right, z_left)
     far = (send_to(z_left, 0, -1), send_to(z_right, 0, 1), send_to(z_over, 0, 2))
-    basis, part, gram = together(mode_work, fields, vectors, weights, scale)
-    part, *far = barrier((part, *far))
+    basis, part, gram, near = together(
+        mode_work, fields, vectors, weights, scale, left, right, *near
+    )
+    part, near, *far = barrier((part, near, *far))
 
     scales = part[:, :, cells:].reshape(8, rows)
     mode = spread(jnp.sum(part[:, :, :cells], axis=0).astype(BF16), RUNS)
-    keep, send = blocks_of(spot, left, right, *near, z_left, z_right, *far)
+    keep, send = blocks_of(far_kernel, spot, left, right, z_left, z_right, *far)
     blocks = (keep.astype(F32) + swap_cores(send).astype(F32)).astype(BF16)
     gram_keep = jnp.where(core == 0, gram[:4], gram[4:])
     gram_send = jnp.where(core == 0, gram[4:], gram[:4])
     gram = (gram_keep + swap_cores(gram_send)).astype(BF16)
     mode = mode.reshape(common, cells)
     mode_wide = mode.astype(F32)
-    norms = jnp.sum(mode_wide * mode_wide, axis=1) / total
-    norms = jnp.concatenate([norms, norms])[None]
-    pcs = pcs_of(fields, mode, norms)
+    pcs = pcs_of(fields, mode)
     pcs_keep = jnp.where(core == 0, pcs[:2], pcs[2:])
     pcs_send = jnp.where(core == 0, pcs[2:], pcs[:2])
     pcs = split(pcs_keep + swap_cores(pcs_send))
     extra = jnp.concatenate([gram, pcs], axis=0)
     extra = extra.reshape(8, 4, 32, 128).transpose(1, 0, 2, 3).reshape(4, 256, 128)
 
-    half = rows * 3
-    blocks = scatter_x(jnp.concatenate([blocks.reshape(4, half, 128), extra], axis=1))
-    extra, blocks = blocks[half:], blocks[:half].astype(BF16).reshape(8, half // 8, 128)
+    half = rows * 3 // 2
+    far = scatter_x(jnp.concatenate([blocks.reshape(4, half, 128), extra], axis=1))
+    extra, far = far[half:], far[:half].astype(BF16)
+    blocks = jnp.where(a == 0, jnp.concatenate([near, far]), jnp.concatenate([far, near]))
+    blocks = blocks.reshape(8, half // 4, 128)
     others = lax.all_to_all(blocks, RUNS, 0, 0, tiled=True)
     same = lax.broadcasted_iota(jnp.int32, (8, 1, 1), 0) == a * 4 + b
     others = jnp.where(same, 0.0, others.astype(F32))
-    blocks = (blocks.astype(F32) + others).astype(BF16).reshape(4, half // 4, 128)
+    blocks = (blocks.astype(F32) + others).astype(BF16).reshape(4, half // 2, 128)
     pcs = split(extra[128:192] + extra[192:]).reshape(2, 4, 16, 128)
     pieces = [blocks, extra[:128].astype(BF16).reshape(4, 32, 128), pcs[0], pcs[1]]
     pieces = jnp.concatenate(pieces, axis=1)
@@ -356,10 +370,11 @@
         for n in range(2)
     )
     gram = gram[:, :months, :months] / total
-    inverse = lax.rsqrt(pcs[0, months])
-    pcs = pcs[:, :months] * inverse / total
-    pcs = jnp.concatenate([pcs[:, :, :common], pcs[:, :, common:]], axis=0)
-    eofs = (mode_wide * inverse[:common, None]).astype(BF16)
+    pcs = pcs.reshape(runs // 2, 2, common, 128)
+    inverse = lax.rsqrt(pcs[0, 0, :, months : months + 1] / total)
+    pcs = (pcs[..., :months] * (inverse / total)).transpose(1, 0, 2, 3)
+    pcs = pcs.reshape(runs, common, months).swapaxes(1, 2)
+    eofs = (mode_wide * inverse).astype(BF16)
     return (gram, basis, merged, eofs, pcs)
 
 

time: 226 us -> 219 us (0.969)
  blocking collectives: 103 us -> 81.6 us
  starting transfers between devices: 32.7 us -> 44 us
  other arithmetic: 10.2 us -> 13.7 us
  local copies, waits for them, and re-layouts: 10.1 us -> 7.48 us
    all_to_all x1 -> x0, blocking collectives: 21.6 us -> none  [scatter_x(): return sum_of(lax.all_to_all(parts, 'x', 0, 0, tiled=True))]
    all_to_all x1, waiting for transfers between devices: 21.4 us -> 0.01 us  [mode_work(): part = lax.all_to_all(part, RUNS, 0, 0, tiled=True)]
    all_to_all x0 -> x2, waiting for transfers between devices: none -> 20.4 us  [scatter_x(): return sum_of(lax.all_to_all(parts, 'x', 0, 0, tiled=True))]
    all_to_all x0 -> x2, starting transfers between devices: none -> 7.66 us  [scatter_x(): return sum_of(lax.all_to_all(parts, 'x', 0, 0, tiled=True))]
    ppermute x4 -> x5, starting transfers between devices: 8.2 us -> 11 us  [swap_cores(): return lax.ppermute(x, 'core', [(0, 1), (1, 0)])]
    pallas_call x1 -> x2, Pallas kernels: 9.86 us -> 11.6 us  [blocks_of(): pl.pallas_call(kernel, in_specs=[pl.BlockSpec(memory_space=pltpu.SMEM)] +...]
  transfers between devices with their start and end apart: 15 -> 18, of which waited for: 3 -> 5; matrix products, arithmetic and copies ran while one was open for 6% -> 8% of each run, Pallas kernels for 9% -> 10%
where the time goes in v2:
time: 219 us; the launch traced here: 218 us
  blocking collectives  81.6 us (37%)
  starting transfers between devices  44 us (20%)
  Pallas kernels  34.6 us (16%)
  waiting for transfers between devices  29.1 us (13%)
  other arithmetic  13.7 us (6%)
  local copies, waits for them, and re-layouts  7.48 us (3%)
  matrix products  6.03 us (3%)
    all_to_all x3, blocking collectives, spread(): lax.all_to_all(jnp.broadcast_to(x[None], (n,) + x.shape), axes, 0, 0, til...  69.7 us
    all_to_all x2, waiting for transfers between devices, scatter_x(): return sum_of(lax.all_to_all(parts, 'x', 0, 0, tiled=True))  20.4 us
    all_to_all x1, blocking collectives, per_device(): pieces = sum_of(lax.all_to_all(pieces, 'z_hi', 0, 0, tiled=True))  11.9 us
    pallas_call x2, Pallas kernels, blocks_of(): pl.pallas_call(kernel, in_specs=[pl.BlockSpec(memory_space=pltpu.SMEM)] +...  11.6 us
    ppermute x8, starting transfers between devices, send_to(): return lax.ppermute(x, RUNS, pairs)  11.4 us
    ppermute x5, starting transfers between devices, swap_cores(): return lax.ppermute(x, 'core', [(0, 1), (1, 0)])  11 us
    all_to_all x2, starting transfers between devices, scatter_x(): return sum_of(lax.all_to_all(parts, 'x', 0, 0, tiled=True))  7.66 us
    pallas_call x1, Pallas kernels, project(): pl.pallas_call(project_kernel, grid_spec=pltpu.PrefetchScalarGridSpec(num...  7.25 us
  transfers between devices with their start and end apart: 18, of which 5 were waited for; matrix products, arithmetic and copies ran while one was open for 8% of the time, Pallas kernels for 10%

profile of v2, /device:TPU:1, one launch (start us, length us, event | category | flops | bytes accessed | tf_op | source)
XLA Modules:
  0.0 217.6 jit_solution(16030561339721883058)
XLA Ops:
  0.6 1.1 copy.40.vectors
  1.8 7.2 %shard_map.75 = (bf16[384,1024]{1,0:T(8,128)(2,1)S(1)}, bf16[384,1024]{1,0:T(8,128)(2,1)}, bf16[384,1024]{1,0:T(8,128)(2,1)S(1)}, f32[8,48,1]{2,1,0:T(8,128)S(1)}) custom-call(s32[3]{0:T(128)S(1)} %pad_add_fusion.spot, bf16[8,120,2048]{2,1,0:T(8,128)(2,1)} %second.1, bf16[8,120,48]{2,1,0:T(8,128)(2,1)S(1)} %copy.40.vectors), custom_call_target="tpu_custom_call" | custom-call | flops 188743680 | bytes 7864320 | tf_op jit(solution)/shard_map/pallas_call | solution.py:55
  9.0 2.5 %collective-permute-start.1 = (bf16[384,1024]{1,0:T(8,128)(2,1)S(1)}, bf16[384,1024]{1,0:T(8,128)(2,1)S(1)}, u32[]{:S(2)}, u32[]{:S(2)}) collective-permute-start(bf16[384,1024]{1,0:T(8,128)(2,1)S(1)} %get-tuple-element.82.left), channel_id=1, source_target_pairs={{0,128},{32,160},{64,192},{96,224},{128,0},{160,32},{192,64},{224,... | collective-permute-start | bytes 2359304 | tf_op jit(solution)/shard_map/ppermute | solution.py:20
  11.5 2.7 %collective-permute-start.3 = (bf16[384,1024]{1,0:T(8,128)(2,1)S(1)}, bf16[384,1024]{1,0:T(8,128)(2,1)}, u32[]{:S(2)}, u32[]{:S(2)}) collective-permute-start(bf16[384,1024]{1,0:T(8,128)(2,1)S(1)} %get-tuple-element.82.left), channel_id=1, source_target_pairs={{0,96},{32,0},{64,32},{96,64},{128,224},{160,128},{192,160},{224,1... | collective-permute-start | bytes 2359304 | tf_op jit(solution)/shard_map/ppermute | solution.py:20
  14.3 1.6 collective-permute-start.5
  16.0 40.1 %conditional.2 = (f32[8,48]{1,0:T(8,128)S(1)}) conditional(s32[]{:T(128)} %convert_element_type.85, () %tuple.31, f32[8,48,1]{2,1,0:T(8,128)S(1)} %get-tuple-element.81), branch_computations={%region_0.0_spmd, %region_1.0_spmd} | conditional | flops 12288 | bytes 211984 | solution.py:276
  16.2 39.7 %all_to_all.42 = f32[32,3,128]{2,1,0:T(4,128)S(1)} all-to-all(f32[32,3,128]{2,1,0:T(4,128)S(1)} %broadcast_in_dim.21), channel_id=1, replica_groups=mesh['z_lo'=2,'y'=4,'x'=4,'z_hi'=4,'core'=2] {'x','z_hi','core'}, dimensions={0} | all-to-all | bytes 98304 | tf_op jit(solution)/shard_map/cond/branch_1_fun/all_to_all | solution.py:29
  56.1 2.8 %collective-permute-start.6 = (bf16[384,1024]{1,0:T(8,128)(2,1)S(1)}, bf16[384,1024]{1,0:T(8,128)(2,1)S(1)}, u32[]{:S(2)}, u32[]{:S(2)}) collective-permute-start(bf16[384,1024]{1,0:T(8,128)(2,1)S(1)} %collective-permute-done.1.z_left), channel_id=1, source_target_pairs={{0,96},{32,0},{64,32},{96,64},{128,224},{160,128},{192,160},{224,1... | collective-permute-start | bytes 2359304 | tf_op jit(solution)/shard_map/ppermute | solution.py:20
  58.9 1.0 broadcast_select_fusion
  59.9 1.6 collective-permute-start.8
  61.6 43.2 %conditional.3 = (bf16[384,2048]{1,0:T(8,128)(2,1)}, f32[8,8,2096]{2,1,0:T(8,128)}, f32[8,128,128]{2,1,0:T(8,128)}, bf16[576,128]{1,0:T(8,128)(2,1)S(1)}, f32[4,...) conditional(s32[]{:T(128)} %convert_element_type.85, () %tuple.30, (bf16[8,120,48]{1,2,0:T(8,128)(2,1)}, ...), branch_computations={%region_3.4_spmd, %region_4.6_spmd} | conditional | flops 2123328512 | bytes 31908128 | solution.py:276
  61.6 6.2 %branch_1_fun.2 = (bf16[4,12,48,128]{3,2,1,0:T(8,128)(2,1)S(1)}, bf16[4,12,48,128]{3,2,1,0:T(8,128)(2,1)}) custom-call(s32[3]{0:T(128)} %get-tuple-element.44.spot, bf16[384,1024]{1,0:T(8,128)(2,1)} %get-tuple-element.45.left, bf16[384,1024]{1,0:T(8,128)(2,1)} %get-tuple-element.46.right, bf16[384,1024]{1,0:T(8,128)(2,1)} %get-tuple-element.47.down, ...), custom_call_target="tpu_custom_call" | custom-call | flops 1358954496 | bytes 4718592 | tf_op jit(solution)/shard_map/cond/branch_1_fun/pallas_call | solution.py:202
  67.8 0.8 copy-done.2
  68.6 1.2 collective-permute-start
  69.8 4.2 %multiply_convert_fusion = bf16[8,48,2048]{2,1,0:T(8,128)(2,1)} fusion(bf16[8,120,48]{1,2,0:T(8,128)(2,1)S(1)} %copy-done.7, bf16[8,120,2048]{2,1,0:T(8,128)(2,1)} %get-tuple-element.40.fields, f32[8,48]{1,0:T(8,128)S(1)} %rsqrt.26), kind=kOutput, calls=%fused_computation | convolution fusion | flops 190316544 | bytes 5598720 | tf_op jit(solution)/shard_map/cond/branch_1_fun/rmk,rmc->rkc/dot_general | solution.py:302
  74.0 2.0 add_convert_fusion
  76.1 4.2 %all-to-all-start.1 = ((bf16[4,576,128]{2,1,0:T(8,128)(2,1)}), bf16[4,576,128]{2,1,0:T(8,128)(2,1)}, u32[]{:S(2)}, u32[]{:S(2)}) async-start(bf16[4,576,128]{2,1,0:T(8,128)(2,1)} %bitcast.48), calls=%async_computation.1 | async-start | bytes 1179648 | tf_op jit(solution)/shard_map/cond/branch_1_fun/all_to_all | solution.py:269
  80.2 1.8 fusion
  82.1 0.8 pad_maximum_fusion
  82.9 7.7 %all-to-all-done.1 = bf16[4,576,128]{2,1,0:T(8,128)(2,1)} async-done(((bf16[4,576,128]{2,1,0:T(8,128)(2,1)}), bf16[4,576,128]{2,1,0:T(8,128)(2,1)}, u32[]{:S(2)}, u32[]{:S(2)}) %all-to-all-start.1) | async-done | bytes 589856 | tf_op jit(solution)/shard_map/cond/branch_1_fun/all_to_all | solution.py:269
  90.6 1.2 reduce_sum.44
  91.8 4.4 %all-to-all-start.2 = ((f32[8,8,2096]{2,1,0:T(8,128)}), f32[8,8,2096]{2,1,0:T(8,128)}, u32[]{:S(2)}, u32[]{:S(2)}) async-start(f32[8,8,2096]{2,1,0:T(8,128)} %pad_maximum_fusion), calls=%async_computation.2 | async-start | bytes 1114112 | tf_op jit(solution)/shard_map/cond/branch_1_fun/all_to_all | solution.py:307
  96.2 6.8 %branch_1_fun.3 = f32[8,128,128]{2,1,0:T(8,128)} custom-call(bf16[8,120,2048]{2,1,0:T(8,128)(2,1)} %get-tuple-element.40.fields), custom_call_target="tpu_custom_call" | custom-call | flops 471859200 | bytes 3932160 | tf_op jit(solution)/shard_map/cond/branch_1_fun/pallas_call | solution.py:84
  103.0 1.8 fusion.12
  104.7 0.8 broadcast_select_fusion.1
  105.5 3.0 %collective-permute-start.10 = (f32[4,128,128]{2,1,0:T(8,128)}, f32[4,128,128]{2,1,0:T(8,128)}, u32[]{:S(2)}, u32[]{:S(2)}) collective-permute-start(f32[4,128,128]{2,1,0:T(8,128)} %broadcast_select_fusion.1), channel_id=1, source_target_pairs={{0,1},{1,0},{2,3},{3,2},{4,5},{5,4},{6,7},{7,6},{8,9},{9,8},{10,11... | collective-permute-start | bytes 786440 | tf_op jit(solution)/shard_map/ppermute | solution.py:24
  108.5 1.1 slice_reduce_fusion
  110.3 3.9 %all-to-all-start.3 = ((bf16[8,8,2048]{2,1,0:T(8,128)(2,1)}), bf16[8,8,2048]{2,1,0:T(8,128)(2,1)S(1)}, u32[]{:S(2)}, u32[]{:S(2)}) async-start(bf16[8,8,2048]{2,1,0:T(8,128)(2,1)} %broadcast_in_dim.32), calls=%async_computation.3 | async-start | bytes 524288 | tf_op jit(solution)/shard_map/all_to_all | solution.py:29
  114.3 5.4 %shard_map.76 = (bf16[4,12,48,128]{3,2,1,0:T(8,128)(2,1)S(1)}, bf16[4,12,48,128]{3,2,1,0:T(8,128)(2,1)}) custom-call(s32[3]{0:T(128)} %copy-done.10, bf16[384,1024]{1,0:T(8,128)(2,1)} %copy-done.6, bf16[384,1024]{1,0:T(8,128)(2,1)} %get-tuple-element.83.right, bf16[384,1024]{1,0:T(8,128)(2,1)S(1)} %collective-permute-done.1.z_left, ...), custom_call_target="tpu_custom_call" | custom-call | flops 1358954496 | bytes 4718592 | tf_op jit(solution)/shard_map/pallas_call | solution.py:202
  119.7 0.8 copy-done
  120.8 1.1 add_convert_fusion.3
  121.9 4.0 %shard_map.77 = f32[4,128,128]{2,1,0:T(8,128)S(1)} custom-call(bf16[8,120,2048]{2,1,0:T(8,128)(2,1)} %second.1, bf16[8,120,2048]{2,1,0:T(8,128)(2,1)} %second.1, bf16[64,2048]{1,0:T(8,128)(2,1)S(1)} %bitcast.46), custom_call_target="tpu_custom_call" | custom-call | flops 251658240 | bytes 3932160 | tf_op jit(solution)/shard_map/pallas_call | solution.py:112
  126.5 0.8 collective-permute-done.11
  127.5 1.0 pad_maximum_fusion.1
  128.4 3.5 %all-to-all-start.4 = ((bf16[4,832,128]{2,1,0:T(8,128)(2,1)}), bf16[4,832,128]{2,1,0:T(8,128)(2,1)S(1)}, u32[]{:S(2)}, u32[]{:S(2)}) async-start(bf16[4,832,128]{2,1,0:T(8,128)(2,1)} %pad_maximum_fusion.1), calls=%async_computation.4 | async-start | bytes 1703936 | tf_op jit(solution)/shard_map/all_to_all | solution.py:269
  132.0 12.7 %all-to-all-done.4 = bf16[4,832,128]{2,1,0:T(8,128)(2,1)S(1)} async-done(((bf16[4,832,128]{2,1,0:T(8,128)(2,1)}), bf16[4,832,128]{2,1,0:T(8,128)(2,1)S(1)}, u32[]{:S(2)}, u32[]{:S(2)}) %all-to-all-start.4) | async-done | bytes 852000 | tf_op jit(solution)/shard_map/all_to_all | solution.py:269
  144.8 0.8 maximum_select_fusion
  145.6 5.6 %all-to-all-start.5 = ((bf16[8,144,128]{2,1,0:T(8,128)(2,1)}), bf16[8,144,128]{2,1,0:T(8,128)(2,1)S(1)}, u32[]{:S(2)}, u32[]{:S(2)}) async-start(bf16[8,144,128]{2,1,0:T(8,128)(2,1)} %bitcast.13), calls=%async_computation.5 | async-start | bytes 589824 | tf_op jit(solution)/shard_map/all_to_all | solution.py:340
  151.3 6.2 %all-to-all-done.5 = bf16[8,144,128]{2,1,0:T(8,128)(2,1)S(1)} async-done(((bf16[8,144,128]{2,1,0:T(8,128)(2,1)}), bf16[8,144,128]{2,1,0:T(8,128)(2,1)S(1)}, u32[]{:S(2)}, u32[]{:S(2)}) %all-to-all-start.5) | async-done | bytes 294944 | tf_op jit(solution)/shard_map/all_to_all | solution.py:340
  157.5 1.1 add_convert_fusion.2
  158.6 11.9 %all_to_all.43 = bf16[4,352,128]{2,1,0:T(8,128)(2,1)S(1)} all-to-all(bf16[4,352,128]{2,1,0:T(8,128)(2,1)S(1)} %pad_maximum_fusion.4), channel_id=1, replica_groups=mesh['z_lo'=2,'y'=4,'x'=4,'z_hi'=4,'core'=2] {'z_hi'}, dimensions={0} | all-to-all | bytes 720896 | tf_op jit(solution)/shard_map/all_to_all | solution.py:347
  170.7 13.3 %all_to_all.44 = bf16[4,352,128]{2,1,0:T(8,128)(2,1)S(1)} all-to-all(bf16[4,352,128]{2,1,0:T(8,128)(2,1)S(1)} %broadcast_in_dim.35), channel_id=1, replica_groups=mesh['z_lo'=2,'y'=4,'x'=4,'z_hi'=4,'core'=2] {'z_hi'}, dimensions={0} | all-to-all | bytes 720896 | tf_op jit(solution)/shard_map/all_to_all | solution.py:29
  184.2 16.7 %all_to_all.45.own = bf16[4,4,352,128]{3,2,1,0:T(8,128)(2,1)S(1)} all-to-all(bf16[4,4,352,128]{3,2,1,0:T(8,128)(2,1)S(1)} %broadcast_in_dim.36), channel_id=1, replica_groups=mesh['z_lo'=2,'y'=4,'x'=4,'z_hi'=4,'core'=2] {'x'}, dimensions={0} | all-to-all | bytes 2883584 | tf_op jit(solution)/shard_map/all_to_all | solution.py:29
  200.9 6.0 %collective-permute-start.12 = (bf16[4,4,352,128]{3,2,1,0:T(8,128)(2,1)S(1)}, bf16[4,4,352,128]{3,2,1,0:T(8,128)(2,1)S(1)}, u32[]{:S(2)}, u32[]{:S(2)}) collective-permute-start(bf16[4,4,352,128]{3,2,1,0:T(8,128)(2,1)S(1)} %all_to_all.45.own), channel_id=1, source_target_pairs={{0,1},{1,0},{2,3},{3,2},{4,5},{5,4},{6,7},{7,6},{8,9},{9,8},{10,11... | collective-permute-start | bytes 4325384 | tf_op jit(solution)/shard_map/ppermute | solution.py:24
  208.0 1.7 collective-permute-done.12.other
  210.9 0.8 fusion.5
  211.7 0.8 multiply_convert_fusion.1
  212.6 5.1 %shard_map.78 = f32[384,3072]{1,0:T(8,128)} custom-call(s32[3]{0:T(128)S(1)} %copy-done.11, bf16[4,4,352,128]{3,2,1,0:T(8,128)(2,1)S(1)} %all_to_all.45.own, bf16[4,4,352,128]{3,2,1,0:T(8,128)(2,1)S(1)} %collective-permute-done.12.other, f32[384,1]{1,0:T(8,128)S(1)} %div.43.row, f32[8,1,384]{2,1,0:T(1,128)S(1)} %rsqrt.34.col), custom_call_target="tpu_custom_call" | custom-call | tf_op jit(solution)/shard_map/pallas_call | solution.py:241
  (87 shorter events, 5.1 us)
Async XLA Ops:
  1.8 7.3 %copy-start.10 = (s32[3]{0:T(128)}, s32[3]{0:T(128)S(1)}, u32[]{:S(2)}) copy-start(s32[3]{0:T(128)S(1)} %pad_add_fusion.spot) | copy-start | bytes 40
  9.0 47.1 %copy-start.6 = (bf16[384,1024]{1,0:T(8,128)(2,1)}, bf16[384,1024]{1,0:T(8,128)(2,1)S(1)}, u32[]{:S(2)}) copy-start(bf16[384,1024]{1,0:T(8,128)(2,1)S(1)} %get-tuple-element.82.left) | copy-start | bytes 2359300
  9.0 47.0 %collective-permute-start.1 = (bf16[384,1024]{1,0:T(8,128)(2,1)S(1)}, bf16[384,1024]{1,0:T(8,128)(2,1)S(1)}, u32[]{:S(2)}, u32[]{:S(2)}) collective-permute-start(bf16[384,1024]{1,0:T(8,128)(2,1)S(1)} %get-tuple-element.82.left), channel_id=1, source_target_pairs={{0,128},{32,160},{64,192},{96,224},{128,0},{160,32},{192,64},{224,... | collective-permute-start | bytes 2359304 | tf_op jit(solution)/shard_map/ppermute | solution.py:20
  11.5 44.6 %collective-permute-start.3 = (bf16[384,1024]{1,0:T(8,128)(2,1)S(1)}, bf16[384,1024]{1,0:T(8,128)(2,1)}, u32[]{:S(2)}, u32[]{:S(2)}) collective-permute-start(bf16[384,1024]{1,0:T(8,128)(2,1)S(1)} %get-tuple-element.82.left), channel_id=1, source_target_pairs={{0,96},{32,0},{64,32},{96,64},{128,224},{160,128},{192,160},{224,1... | collective-permute-start | bytes 2359304 | tf_op jit(solution)/shard_map/ppermute | solution.py:20
  14.2 41.8 %collective-permute-start.2 = (bf16[384,1024]{1,0:T(8,128)(2,1)}, bf16[384,1024]{1,0:T(8,128)(2,1)S(1)}, u32[]{:S(2)}, u32[]{:S(2)}) collective-permute-start(bf16[384,1024]{1,0:T(8,128)(2,1)} %get-tuple-element.83.right), channel_id=1, source_target_pairs={{0,128},{32,160},{64,192},{96,224},{128,0},{160,32},{192,64},{224,... | collective-permute-start | bytes 2359304 | tf_op jit(solution)/shard_map/ppermute | solution.py:20
  14.3 41.8 %collective-permute-start.4 = (bf16[384,1024]{1,0:T(8,128)(2,1)}, bf16[384,1024]{1,0:T(8,128)(2,1)}, u32[]{:S(2)}, u32[]{:S(2)}) collective-permute-start(bf16[384,1024]{1,0:T(8,128)(2,1)} %get-tuple-element.83.right), channel_id=1, source_target_pairs={{0,32},{32,64},{64,96},{96,0},{128,160},{160,192},{192,224},{224,1... | collective-permute-start | bytes 2359304 | tf_op jit(solution)/shard_map/ppermute | solution.py:20
  14.3 41.8 %collective-permute-start.5 = (bf16[384,1024]{1,0:T(8,128)(2,1)S(1)}, bf16[384,1024]{1,0:T(8,128)(2,1)}, u32[]{:S(2)}, u32[]{:S(2)}) collective-permute-start(bf16[384,1024]{1,0:T(8,128)(2,1)S(1)} %get-tuple-element.84), channel_id=1, source_target_pairs={{0,64},{32,96},{64,0},{96,32},{128,192},{160,224},{192,128},{224,1... | collective-permute-start | bytes 2359304 | tf_op jit(solution)/shard_map/ppermute | solution.py:20
  56.1 5.5 %copy-start.8 = (f32[8,48]{1,0:T(8,128)}, f32[8,48]{1,0:T(8,128)S(1)}, u32[]{:S(2)}) copy-start(f32[8,48]{1,0:T(8,128)S(1)} %get-tuple-element.127) | copy-start | bytes 4612
  56.1 52.4 %collective-permute-start.6 = (bf16[384,1024]{1,0:T(8,128)(2,1)S(1)}, bf16[384,1024]{1,0:T(8,128)(2,1)S(1)}, u32[]{:S(2)}, u32[]{:S(2)}) collective-permute-start(bf16[384,1024]{1,0:T(8,128)(2,1)S(1)} %collective-permute-done.1.z_left), channel_id=1, source_target_pairs={{0,96},{32,0},{64,32},{96,64},{128,224},{160,128},{192,160},{224,1... | collective-permute-start | bytes 2359304 | tf_op jit(solution)/shard_map/ppermute | solution.py:20
  58.9 49.6 %collective-permute-start.7 = (bf16[384,1024]{1,0:T(8,128)(2,1)S(1)}, bf16[384,1024]{1,0:T(8,128)(2,1)S(1)}, u32[]{:S(2)}, u32[]{:S(2)}) collective-permute-start(bf16[384,1024]{1,0:T(8,128)(2,1)S(1)} %collective-permute-done.2.z_right), channel_id=1, source_target_pairs={{0,32},{32,64},{64,96},{96,0},{128,160},{160,192},{192,224},{224,1... | collective-permute-start | bytes 2359304 | tf_op jit(solution)/shard_map/ppermute | solution.py:20
  59.9 48.6 %collective-permute-start.8 = (bf16[384,1024]{1,0:T(8,128)(2,1)}, bf16[384,1024]{1,0:T(8,128)(2,1)}, u32[]{:S(2)}, u32[]{:S(2)}) collective-permute-start(bf16[384,1024]{1,0:T(8,128)(2,1)} %broadcast_select_fusion), channel_id=1, source_target_pairs={{0,64},{32,96},{64,0},{96,32},{128,192},{160,224},{192,128},{224,1... | collective-permute-start | bytes 2359304 | tf_op jit(solution)/shard_map/ppermute | solution.py:20
  61.6 8.3 %copy-start.7 = (bf16[8,120,48]{1,2,0:T(8,128)(2,1)S(1)}, bf16[8,120,48]{1,2,0:T(8,128)(2,1)}, u32[]{:S(2)}) copy-start(bf16[8,120,48]{1,2,0:T(8,128)(2,1)} %get-tuple-element.39) | copy-start | bytes 276484 | tf_op jit(solution)/shard_map/cond
  67.7 0.8 copy-start.2
  68.6 5.4 %collective-permute-start = (bf16[4,12,48,128]{3,2,1,0:T(8,128)(2,1)}, bf16[4,12,48,128]{3,2,1,0:T(8,128)(2,1)}, u32[]{:S(2)}, u32[]{:S(2)}) collective-permute-start(bf16[4,12,48,128]{3,2,1,0:T(8,128)(2,1)} %get-tuple-element.51), channel_id=1, source_target_pairs={{0,1},{1,0},{2,3},{3,2},{4,5},{5,4},{6,7},{7,6},{8,9},{9,8},{10,11... | collective-permute-start | bytes 1769480 | tf_op jit(solution)/shard_map/cond/branch_1_fun/ppermute | solution.py:24
  69.8 4.2 %copy-start.3 = (bf16[4,12,48,128]{3,2,1,0:T(8,128)(2,1)S(1)}, bf16[4,12,48,128]{3,2,1,0:T(8,128)(2,1)}, u32[]{:S(2)}) copy-start(bf16[4,12,48,128]{3,2,1,0:T(8,128)(2,1)} %copy-done.2) | copy-start | bytes 1769476 | tf_op jit(solution)/shard_map/cond
  76.1 14.6 %all-to-all-start.1 = ((bf16[4,576,128]{2,1,0:T(8,128)(2,1)}), bf16[4,576,128]{2,1,0:T(8,128)(2,1)}, u32[]{:S(2)}, u32[]{:S(2)}) async-start(bf16[4,576,128]{2,1,0:T(8,128)(2,1)} %bitcast.48), calls=%async_computation.1 | async-start | bytes 1179648 | tf_op jit(solution)/shard_map/cond/branch_1_fun/all_to_all | solution.py:269
  91.8 12.9 %all-to-all-start.2 = ((f32[8,8,2096]{2,1,0:T(8,128)}), f32[8,8,2096]{2,1,0:T(8,128)}, u32[]{:S(2)}, u32[]{:S(2)}) async-start(f32[8,8,2096]{2,1,0:T(8,128)} %pad_maximum_fusion), calls=%async_computation.2 | async-start | bytes 1114112 | tf_op jit(solution)/shard_map/cond/branch_1_fun/all_to_all | solution.py:307
  104.7 5.6 %copy-start.4 = (f32[4,128,128]{2,1,0:T(8,128)}, f32[4,128,128]{2,1,0:T(8,128)S(1)}, u32[]{:S(2)}) copy-start(f32[4,128,128]{2,1,0:T(8,128)S(1)} %get-tuple-element.99) | copy-start | bytes 786436
  105.5 15.2 %collective-permute-start.10 = (f32[4,128,128]{2,1,0:T(8,128)}, f32[4,128,128]{2,1,0:T(8,128)}, u32[]{:S(2)}, u32[]{:S(2)}) collective-permute-start(f32[4,128,128]{2,1,0:T(8,128)} %broadcast_select_fusion.1), channel_id=1, source_target_pairs={{0,1},{1,0},{2,3},{3,2},{4,5},{5,4},{6,7},{7,6},{8,9},{9,8},{10,11... | collective-permute-start | bytes 786440 | tf_op jit(solution)/shard_map/ppermute | solution.py:24
  110.3 11.5 %all-to-all-start.3 = ((bf16[8,8,2048]{2,1,0:T(8,128)(2,1)}), bf16[8,8,2048]{2,1,0:T(8,128)(2,1)S(1)}, u32[]{:S(2)}, u32[]{:S(2)}) async-start(bf16[8,8,2048]{2,1,0:T(8,128)(2,1)} %broadcast_in_dim.32), calls=%async_computation.3 | async-start | bytes 524288 | tf_op jit(solution)/shard_map/all_to_all | solution.py:29
  114.2 6.5 %copy-start.5 = (f32[4,128,128]{2,1,0:T(8,128)S(1)}, f32[4,128,128]{2,1,0:T(8,128)}, u32[]{:S(2)}) copy-start(f32[4,128,128]{2,1,0:T(8,128)} %copy-done.4) | copy-start | bytes 786436
  119.7 0.8 copy-start
  120.5 5.9 %collective-permute-start.9 = (bf16[4,12,48,128]{3,2,1,0:T(8,128)(2,1)}, bf16[4,12,48,128]{3,2,1,0:T(8,128)(2,1)S(1)}, u32[]{:S(2)}, u32[]{:S(2)}) collective-permute-start(bf16[4,12,48,128]{3,2,1,0:T(8,128)(2,1)} %get-tuple-element.98), channel_id=1, source_target_pairs={{0,1},{1,0},{2,3},{3,2},{4,5},{5,4},{6,7},{7,6},{8,9},{9,8},{10,11... | collective-permute-start | bytes 1769480 | tf_op jit(solution)/shard_map/ppermute | solution.py:24
  121.9 4.5 %copy-start.1 = (bf16[4,12,48,128]{3,2,1,0:T(8,128)(2,1)S(1)}, bf16[4,12,48,128]{3,2,1,0:T(8,128)(2,1)}, u32[]{:S(2)}) copy-start(bf16[4,12,48,128]{3,2,1,0:T(8,128)(2,1)} %copy-done) | copy-start | bytes 1769476
  125.9 1.5 collective-permute-start.11
  128.4 16.2 %all-to-all-start.4 = ((bf16[4,832,128]{2,1,0:T(8,128)(2,1)}), bf16[4,832,128]{2,1,0:T(8,128)(2,1)S(1)}, u32[]{:S(2)}, u32[]{:S(2)}) async-start(bf16[4,832,128]{2,1,0:T(8,128)(2,1)} %pad_maximum_fusion.1), calls=%async_computation.4 | async-start | bytes 1703936 | tf_op jit(solution)/shard_map/all_to_all | solution.py:269
  145.6 11.8 %all-to-all-start.5 = ((bf16[8,144,128]{2,1,0:T(8,128)(2,1)}), bf16[8,144,128]{2,1,0:T(8,128)(2,1)S(1)}, u32[]{:S(2)}, u32[]{:S(2)}) async-start(bf16[8,144,128]{2,1,0:T(8,128)(2,1)} %bitcast.13), calls=%async_computation.5 | async-start | bytes 589824 | tf_op jit(solution)/shard_map/all_to_all | solution.py:340
  184.2 22.7 %copy-start.9 = (f32[8,48]{1,0:T(8,128)S(1)}, f32[8,48]{1,0:T(8,128)}, u32[]{:S(2)}) copy-start(f32[8,48]{1,0:T(8,128)} %copy-done.8) | copy-start | bytes 4612
  200.9 8.9 %collective-permute-start.12 = (bf16[4,4,352,128]{3,2,1,0:T(8,128)(2,1)S(1)}, bf16[4,4,352,128]{3,2,1,0:T(8,128)(2,1)S(1)}, u32[]{:S(2)}, u32[]{:S(2)}) collective-permute-start(bf16[4,4,352,128]{3,2,1,0:T(8,128)(2,1)S(1)} %all_to_all.45.own), channel_id=1, source_target_pairs={{0,1},{1,0},{2,3},{3,2},{4,5},{5,4},{6,7},{7,6},{8,9},{9,8},{10,11... | collective-permute-start | bytes 4325384 | tf_op jit(solution)/shard_map/ppermute | solution.py:24
  209.9 2.7 %copy-start.11 = (s32[3]{0:T(128)S(1)}, s32[3]{0:T(128)}, u32[]{:S(2)}) copy-start(s32[3]{0:T(128)} %copy-done.10) | copy-start | bytes 40

commit v3 on v2

--- a/solution.py
+++ b/solution.py
@@ -291,9 +291,12 @@
     z_left, z_right = send_to(left, 1, 0), send_to(right, 1, 0)
     weights = lax.dynamic_slice_in_dim(combos, lax.axis_index(RUNS) * rows, rows, 0)
 
-    def scale_work(squares):
+    def scale_work(fields, squares):
         scale = jnp.sum(spread(squares.reshape(3, rows // 3), CELLS), axis=0)
-        return scale.reshape(runs, modes) / total
+        gram = gram_of(fields)
+        gram_keep = jnp.where(core == 0, gram[:4], gram[4:])
+        gram_send = jnp.where(core == 0, gram[4:], gram[:4])
+        return scale.reshape(runs, modes) / total, gram_keep, gram_send
 
     def mode_work(fields, vectors, weights, scale, left, right, *near):
         keep, send = blocks_of(near_kernel, spot, left, right, *near)
@@ -305,13 +308,13 @@
         part = jnp.concatenate([part, jnp.broadcast_to(scale[None], (8, runs, modes))], axis=2)
         part, blocks = barrier((part, blocks))
         part = lax.all_to_all(part, RUNS, 0, 0, tiled=True)
-        return basis, part, gram_of(fields), blocks
-
-    scale = together(scale_work, squares)
+        return basis, part, blocks
+
+    scale, gram_keep, gram_send = together(scale_work, fields, squares)
     scale, z_left, z_right, *near = barrier((scale, z_left, z_right, *near))
     z_over = jnp.where(b // 2 == 0, z_right, z_left)
     far = (send_to(z_left, 0, -1), send_to(z_right, 0, 1), send_to(z_over, 0, 2))
-    basis, part, gram, near = together(
+    basis, part, near = together(
         mode_work, fields, vectors, weights, scale, left, right, *near
     )
     part, near, *far = barrier((part, near, *far))
@@ -320,8 +323,6 @@
     mode = spread(jnp.sum(part[:, :, :cells], axis=0).astype(BF16), RUNS)
     keep, send = blocks_of(far_kernel, spot, left, right, z_left, z_right, *far)
     blocks = (keep.astype(F32) + swap_cores(send).astype(F32)).astype(BF16)
-    gram_keep = jnp.where(core == 0, gram[:4], gram[4:])
-    gram_send = jnp.where(core == 0, gram[4:], gram[:4])
     gram = (gram_keep + swap_cores(gram_send)).astype(BF16)
     mode = mode.reshape(common, cells)
     mode_wide = mode.astype(F32)

time: 219 us -> 219 us (level)
  blocking collectives: 81.6 us -> 55.4 us
  waiting for transfers between devices: 29.1 us -> 53.2 us
  starting transfers between devices: 44 us -> 49.4 us
    all_to_all x3 -> x2, blocking collectives: 69.7 us -> 30 us  [spread(): lax.all_to_all(jnp.broadcast_to(x[None], (n,) + x.shape), axes, 0, 0, til...]
    all_to_all x1 -> x2, waiting for transfers between devices: 0.01 us -> 24.3 us  [spread(): lax.all_to_all(jnp.broadcast_to(x[None], (n,) + x.shape), axes, 0, 0, til...]
    all_to_all x0 -> x1, blocking collectives: none -> 13.5 us  [mode_work(): part = lax.all_to_all(part, RUNS, 0, 0, tiled=True)]
    all_to_all x1 -> x2, starting transfers between devices: 3.94 us -> 16.4 us  [spread(): lax.all_to_all(jnp.broadcast_to(x[None], (n,) + x.shape), axes, 0, 0, til...]
    all_to_all x1 -> x0, starting transfers between devices: 4.38 us -> none  [mode_work(): part = lax.all_to_all(part, RUNS, 0, 0, tiled=True)]
  transfers between devices with their start and end apart: 18 -> 18, of which waited for: 5 -> 6; matrix products, arithmetic and copies ran while one was open for 8% -> 7% of each run, Pallas kernels for 10% -> 10%
where the time goes in v3:
time: 219 us; the launch traced here: 218 us
  blocking collectives  55.4 us (25%)
  waiting for transfers between devices  53.2 us (24%)
  starting transfers between devices  49.4 us (23%)
  Pallas kernels  33.6 us (15%)
  other arithmetic  11.9 us (5%)
  local copies, waits for them, and re-layouts  7.17 us (3%)
  matrix products  6.03 us (3%)
    all_to_all x2, blocking collectives, spread(): lax.all_to_all(jnp.broadcast_to(x[None], (n,) + x.shape), axes, 0, 0, til...  30 us
    all_to_all x2, waiting for transfers between devices, spread(): lax.all_to_all(jnp.broadcast_to(x[None], (n,) + x.shape), axes, 0, 0, til...  24.3 us
    all_to_all x2, waiting for transfers between devices, scatter_x(): return sum_of(lax.all_to_all(parts, 'x', 0, 0, tiled=True))  19.9 us
    all_to_all x2, starting transfers between devices, spread(): lax.all_to_all(jnp.broadcast_to(x[None], (n,) + x.shape), axes, 0, 0, til...  16.4 us
    all_to_all x1, blocking collectives, mode_work(): part = lax.all_to_all(part, RUNS, 0, 0, tiled=True)  13.5 us
    all_to_all x1, blocking collectives, per_device(): pieces = sum_of(lax.all_to_all(pieces, 'z_hi', 0, 0, tiled=True))  11.9 us
    pallas_call x2, Pallas kernels, blocks_of(): pl.pallas_call(kernel, in_specs=[pl.BlockSpec(memory_space=pltpu.SMEM)] +...  11.5 us
    ppermute x8, starting transfers between devices, send_to(): return lax.ppermute(x, RUNS, pairs)  9.94 us
  transfers between devices with their start and end apart: 18, of which 6 were waited for; matrix products, arithmetic and copies ran while one was open for 7% of the time, Pallas kernels for 10%

profile of v3, /device:TPU:1, one launch (start us, length us, event | category | flops | bytes accessed | tf_op | source)
XLA Modules:
  0.0 217.9 jit_solution(18159387778373815228)
XLA Ops:
  0.6 1.1 copy.40.vectors
  1.8 7.3 %shard_map.75 = (bf16[384,1024]{1,0:T(8,128)(2,1)}, bf16[384,1024]{1,0:T(8,128)(2,1)}, bf16[384,1024]{1,0:T(8,128)(2,1)S(1)}, f32[8,48,1]{2,1,0:T(8,128)S(1)}) custom-call(s32[3]{0:T(128)S(1)} %pad_add_fusion.spot, bf16[8,120,2048]{2,1,0:T(8,128)(2,1)} %second.1, bf16[8,120,48]{2,1,0:T(8,128)(2,1)S(1)} %copy.40.vectors), custom_call_target="tpu_custom_call" | custom-call | flops 188743680 | bytes 7864320 | tf_op jit(solution)/shard_map/pallas_call | solution.py:55
  9.0 3.7 %collective-permute-start.5 = (bf16[384,1024]{1,0:T(8,128)(2,1)S(1)}, bf16[384,1024]{1,0:T(8,128)(2,1)}, u32[]{:S(2)}, u32[]{:S(2)}) collective-permute-start(bf16[384,1024]{1,0:T(8,128)(2,1)S(1)} %get-tuple-element.89), channel_id=1, source_target_pairs={{0,64},{32,96},{64,0},{96,32},{128,192},{160,224},{192,128},{224,1... | collective-permute-start | bytes 2359304 | tf_op jit(solution)/shard_map/ppermute | solution.py:20
  12.8 0.8 collective-permute-start.3
  13.6 1.6 collective-permute-start.1
  15.9 44.1 %conditional.2 = (f32[8,48]{1,0:T(8,128)S(1)}, f32[4,128,128]{2,1,0:T(8,128)S(1)}, f32[4,128,128]{2,1,0:T(8,128)S(1)}) conditional(s32[]{:T(128)} %convert_element_type.85, () %tuple.31, (f32[8,48,1]{2,1,0:T(8,128)S(1)}, s32[]{:T(128)}, bf16[8,120,2048]{2,1,0:T(8,128)(2,1)}) %tuple.32), branch_computations={%region_0.0_spmd, %region_1.3_spmd} | conditional | flops 472002560 | bytes 5274698 | solution.py:276
  16.7 13.0 %all-to-all-start = ((f32[32,3,128]{2,1,0:T(4,128)}), f32[32,3,128]{2,1,0:T(4,128)S(1)}, u32[]{:S(2)}, u32[]{:S(2)}) async-start(f32[32,3,128]{2,1,0:T(4,128)} %broadcast_in_dim.21), calls=%async_computation | async-start | bytes 131072 | tf_op jit(solution)/shard_map/cond/branch_1_fun/all_to_all | solution.py:29
  29.7 5.8 %branch_1_fun.2 = f32[8,128,128]{2,1,0:T(8,128)S(1)} custom-call(bf16[8,120,2048]{2,1,0:T(8,128)(2,1)} %get-tuple-element.41.fields), custom_call_target="tpu_custom_call" | custom-call | flops 471859200 | bytes 3932160 | tf_op jit(solution)/shard_map/cond/branch_1_fun/pallas_call | solution.py:84
  35.6 24.3 %all-to-all-done = f32[32,3,128]{2,1,0:T(4,128)S(1)} async-done(((f32[32,3,128]{2,1,0:T(4,128)}), f32[32,3,128]{2,1,0:T(4,128)S(1)}, u32[]{:S(2)}, u32[]{:S(2)}) %all-to-all-start) | async-done | bytes 49184 | tf_op jit(solution)/shard_map/cond/branch_1_fun/all_to_all | solution.py:29
  60.1 1.0 broadcast_select_fusion
  61.0 1.4 collective-permute-start.8
  62.5 1.7 collective-permute-start.6
  64.1 1.0 collective-permute-start.10
  65.2 42.0 %conditional.3 = (bf16[384,2048]{1,0:T(8,128)(2,1)}, f32[8,8,2096]{2,1,0:T(8,128)S(1)}, bf16[576,128]{1,0:T(8,128)(2,1)S(1)}) conditional(s32[]{:T(128)} %convert_element_type.85, () %tuple.30, (bf16[8,120,48]{1,2,0:T(8,128)(2,1)S(1)}, bf16[8,120,2048]{2,1,0:T(8,128)(2,1)}, f32[8,48]{1,0:T(8,128)S(1)}, s32[]{:T(128)}, bf16[3072,64]{0,1:T(8,128)(2,1)}, ...), branch_computations={%region_3.4_spmd, %region_4.6_spmd} | conditional | flops 1651469312 | bytes 25981132 | solution.py:276
  65.2 6.2 %branch_1_fun.3 = (bf16[4,12,48,128]{3,2,1,0:T(8,128)(2,1)S(1)}, bf16[4,12,48,128]{3,2,1,0:T(8,128)(2,1)}) custom-call(s32[3]{0:T(128)S(1)} %get-tuple-element.47.spot, bf16[384,1024]{1,0:T(8,128)(2,1)} %get-tuple-element.48.left, bf16[384,1024]{1,0:T(8,128)(2,1)} %get-tuple-element.49.right, bf16[384,1024]{1,0:T(8,128)(2,1)} %get-tuple-element.50.down, ...), custom_call_target="tpu_custom_call" | custom-call | flops 1358954496 | bytes 4718592 | tf_op jit(solution)/shard_map/cond/branch_1_fun/pallas_call | solution.py:202
  71.3 0.8 copy-done.2
  72.2 4.2 %multiply_convert_fusion = bf16[8,48,2048]{2,1,0:T(8,128)(2,1)} fusion(bf16[8,120,48]{1,2,0:T(8,128)(2,1)S(1)} %get-tuple-element.42, bf16[8,120,2048]{2,1,0:T(8,128)(2,1)} %get-tuple-element.43, f32[8,48]{1,0:T(8,128)S(1)} %rsqrt.26), kind=kOutput, calls=%fused_computation | convolution fusion | flops 190316544 | bytes 5598720 | tf_op jit(solution)/shard_map/cond/branch_1_fun/rmk,rmc->rkc/dot_general | solution.py:305
  76.4 2.1 add_convert_fusion
  78.4 4.3 %all-to-all-start.1 = ((bf16[4,576,128]{2,1,0:T(8,128)(2,1)}), bf16[4,576,128]{2,1,0:T(8,128)(2,1)}, u32[]{:S(2)}, u32[]{:S(2)}) async-start(bf16[4,576,128]{2,1,0:T(8,128)(2,1)} %bitcast.48), calls=%async_computation.1 | async-start | bytes 1179648 | tf_op jit(solution)/shard_map/cond/branch_1_fun/all_to_all | solution.py:269
  82.8 1.8 fusion
  84.6 0.8 pad_maximum_fusion
  85.5 7.0 %all-to-all-done.1 = bf16[4,576,128]{2,1,0:T(8,128)(2,1)} async-done(((bf16[4,576,128]{2,1,0:T(8,128)(2,1)}), bf16[4,576,128]{2,1,0:T(8,128)(2,1)}, u32[]{:S(2)}, u32[]{:S(2)}) %all-to-all-start.1) | async-done | bytes 589856 | tf_op jit(solution)/shard_map/cond/branch_1_fun/all_to_all | solution.py:269
  92.5 1.2 reduce_sum.44
  93.6 13.5 %all_to_all.42 = f32[8,8,2096]{2,1,0:T(8,128)S(1)} all-to-all(f32[8,8,2096]{2,1,0:T(8,128)} %pad_maximum_fusion), channel_id=1, replica_groups=mesh['z_lo'=2,'y'=4,'x'=4,'z_hi'=4,'core'=2] {'z_lo','y'}, dimensions={0} | all-to-all | bytes 1073152 | tf_op jit(solution)/shard_map/cond/branch_1_fun/all_to_all | solution.py:310
  107.1 0.8 copy-done.4
  108.7 3.4 %all-to-all-start.3 = ((bf16[8,8,2048]{2,1,0:T(8,128)(2,1)}), bf16[8,8,2048]{2,1,0:T(8,128)(2,1)S(1)}, u32[]{:S(2)}, u32[]{:S(2)}) async-start(bf16[8,8,2048]{2,1,0:T(8,128)(2,1)} %broadcast_in_dim.32), calls=%async_computation.3 | async-start | bytes 524288 | tf_op jit(solution)/shard_map/all_to_all | solution.py:29
  112.1 5.3 %shard_map.76 = (bf16[4,12,48,128]{3,2,1,0:T(8,128)(2,1)S(1)}, bf16[4,12,48,128]{3,2,1,0:T(8,128)(2,1)}) custom-call(s32[3]{0:T(128)} %copy-done.10, bf16[384,1024]{1,0:T(8,128)(2,1)} %get-tuple-element.87.left, bf16[384,1024]{1,0:T(8,128)(2,1)} %get-tuple-element.88.right, bf16[384,1024]{1,0:T(8,128)(2,1)S(1)} %collective-permute-done.1.z_left, ...), custom_call_target="tpu_custom_call" | custom-call | flops 1358954496 | bytes 4718592 | tf_op jit(solution)/shard_map/pallas_call | solution.py:202
  117.5 0.8 copy-done
  118.3 2.7 %collective-permute-start.9 = (bf16[4,12,48,128]{3,2,1,0:T(8,128)(2,1)}, bf16[4,12,48,128]{3,2,1,0:T(8,128)(2,1)S(1)}, u32[]{:S(2)}, u32[]{:S(2)}) collective-permute-start(bf16[4,12,48,128]{3,2,1,0:T(8,128)(2,1)} %get-tuple-element.103), channel_id=1, source_target_pairs={{0,1},{1,0},{2,3},{3,2},{4,5},{5,4},{6,7},{7,6},{8,9},{9,8},{10,11... | collective-permute-start | bytes 1769480 | tf_op jit(solution)/shard_map/ppermute | solution.py:24
  121.0 1.1 add_convert_fusion.3
  122.1 4.0 %shard_map.77 = f32[4,128,128]{2,1,0:T(8,128)S(1)} custom-call(bf16[8,120,2048]{2,1,0:T(8,128)(2,1)} %second.1, bf16[8,120,2048]{2,1,0:T(8,128)(2,1)} %second.1, bf16[64,2048]{1,0:T(8,128)(2,1)S(1)} %bitcast.46), custom_call_target="tpu_custom_call" | custom-call | flops 251658240 | bytes 3932160 | tf_op jit(solution)/shard_map/pallas_call | solution.py:112
  126.4 1.1 collective-permute-done.11
  127.7 1.0 pad_maximum_fusion.1
  128.7 3.5 %all-to-all-start.4 = ((bf16[4,832,128]{2,1,0:T(8,128)(2,1)}), bf16[4,832,128]{2,1,0:T(8,128)(2,1)S(1)}, u32[]{:S(2)}, u32[]{:S(2)}) async-start(bf16[4,832,128]{2,1,0:T(8,128)(2,1)} %pad_maximum_fusion.1), calls=%async_computation.4 | async-start | bytes 1703936 | tf_op jit(solution)/shard_map/all_to_all | solution.py:269
  132.2 12.9 %all-to-all-done.4 = bf16[4,832,128]{2,1,0:T(8,128)(2,1)S(1)} async-done(((bf16[4,832,128]{2,1,0:T(8,128)(2,1)}), bf16[4,832,128]{2,1,0:T(8,128)(2,1)S(1)}, u32[]{:S(2)}, u32[]{:S(2)}) %all-to-all-start.4) | async-done | bytes 852000 | tf_op jit(solution)/shard_map/all_to_all | solution.py:269
  145.3 0.8 maximum_select_fusion
  146.1 5.3 %all-to-all-start.5 = ((bf16[8,144,128]{2,1,0:T(8,128)(2,1)}), bf16[8,144,128]{2,1,0:T(8,128)(2,1)S(1)}, u32[]{:S(2)}, u32[]{:S(2)}) async-start(bf16[8,144,128]{2,1,0:T(8,128)(2,1)} %bitcast.13), calls=%async_computation.5 | async-start | bytes 589824 | tf_op jit(solution)/shard_map/all_to_all | solution.py:341
  151.5 6.2 %all-to-all-done.5 = bf16[8,144,128]{2,1,0:T(8,128)(2,1)S(1)} async-done(((bf16[8,144,128]{2,1,0:T(8,128)(2,1)}), bf16[8,144,128]{2,1,0:T(8,128)(2,1)S(1)}, u32[]{:S(2)}, u32[]{:S(2)}) %all-to-all-start.5) | async-done | bytes 294944 | tf_op jit(solution)/shard_map/all_to_all | solution.py:341
  157.6 1.1 add_convert_fusion.2
  158.8 11.9 %all_to_all.43 = bf16[4,352,128]{2,1,0:T(8,128)(2,1)S(1)} all-to-all(bf16[4,352,128]{2,1,0:T(8,128)(2,1)S(1)} %pad_maximum_fusion.4), channel_id=1, replica_groups=mesh['z_lo'=2,'y'=4,'x'=4,'z_hi'=4,'core'=2] {'z_hi'}, dimensions={0} | all-to-all | bytes 720896 | tf_op jit(solution)/shard_map/all_to_all | solution.py:348
  170.8 13.4 %all_to_all.44 = bf16[4,352,128]{2,1,0:T(8,128)(2,1)S(1)} all-to-all(bf16[4,352,128]{2,1,0:T(8,128)(2,1)S(1)} %broadcast_in_dim.35), channel_id=1, replica_groups=mesh['z_lo'=2,'y'=4,'x'=4,'z_hi'=4,'core'=2] {'z_hi'}, dimensions={0} | all-to-all | bytes 720896 | tf_op jit(solution)/shard_map/all_to_all | solution.py:29
  184.5 16.6 %all_to_all.45.own = bf16[4,4,352,128]{3,2,1,0:T(8,128)(2,1)S(1)} all-to-all(bf16[4,4,352,128]{3,2,1,0:T(8,128)(2,1)S(1)} %broadcast_in_dim.36), channel_id=1, replica_groups=mesh['z_lo'=2,'y'=4,'x'=4,'z_hi'=4,'core'=2] {'x'}, dimensions={0} | all-to-all | bytes 2883584 | tf_op jit(solution)/shard_map/all_to_all | solution.py:29
  201.1 6.1 %collective-permute-start.12 = (bf16[4,4,352,128]{3,2,1,0:T(8,128)(2,1)S(1)}, bf16[4,4,352,128]{3,2,1,0:T(8,128)(2,1)S(1)}, u32[]{:S(2)}, u32[]{:S(2)}) collective-permute-start(bf16[4,4,352,128]{3,2,1,0:T(8,128)(2,1)S(1)} %all_to_all.45.own), channel_id=1, source_target_pairs={{0,1},{1,0},{2,3},{3,2},{4,5},{5,4},{6,7},{7,6},{8,9},{9,8},{10,11... | collective-permute-start | bytes 4325384 | tf_op jit(solution)/shard_map/ppermute | solution.py:24
  207.3 0.8 slice_rsqrt_fusion
  208.3 1.7 collective-permute-done.12.other
  211.2 0.8 fusion.5
  212.0 0.8 multiply_convert_fusion.1
  212.8 5.1 %shard_map.78 = f32[384,3072]{1,0:T(8,128)} custom-call(s32[3]{0:T(128)S(1)} %copy-done.12, bf16[4,4,352,128]{3,2,1,0:T(8,128)(2,1)S(1)} %all_to_all.45.own, bf16[4,4,352,128]{3,2,1,0:T(8,128)(2,1)S(1)} %collective-permute-done.12.other, f32[384,1]{1,0:T(8,128)S(1)} %div.43.row, f32[8,1,384]{2,1,0:T(1,128)S(1)} %rsqrt.34.col), custom_call_target="tpu_custom_call" | custom-call | tf_op jit(solution)/shard_map/pallas_call | solution.py:241
  (88 shorter events, 5.0 us)
Async XLA Ops:
  1.8 7.3 %copy-start.10 = (s32[3]{0:T(128)}, s32[3]{0:T(128)S(1)}, u32[]{:S(2)}) copy-start(s32[3]{0:T(128)S(1)} %pad_add_fusion.spot) | copy-start | bytes 40
  9.0 51.0 %collective-permute-start.5 = (bf16[384,1024]{1,0:T(8,128)(2,1)S(1)}, bf16[384,1024]{1,0:T(8,128)(2,1)}, u32[]{:S(2)}, u32[]{:S(2)}) collective-permute-start(bf16[384,1024]{1,0:T(8,128)(2,1)S(1)} %get-tuple-element.89), channel_id=1, source_target_pairs={{0,64},{32,96},{64,0},{96,32},{128,192},{160,224},{192,128},{224,1... | collective-permute-start | bytes 2359304 | tf_op jit(solution)/shard_map/ppermute | solution.py:20
  12.8 47.2 %collective-permute-start.3 = (bf16[384,1024]{1,0:T(8,128)(2,1)}, bf16[384,1024]{1,0:T(8,128)(2,1)}, u32[]{:S(2)}, u32[]{:S(2)}) collective-permute-start(bf16[384,1024]{1,0:T(8,128)(2,1)} %get-tuple-element.87.left), channel_id=1, source_target_pairs={{0,96},{32,0},{64,32},{96,64},{128,224},{160,128},{192,160},{224,1... | collective-permute-start | bytes 2359304 | tf_op jit(solution)/shard_map/ppermute | solution.py:20
  13.6 46.5 %collective-permute-start.1 = (bf16[384,1024]{1,0:T(8,128)(2,1)}, bf16[384,1024]{1,0:T(8,128)(2,1)S(1)}, u32[]{:S(2)}, u32[]{:S(2)}) collective-permute-start(bf16[384,1024]{1,0:T(8,128)(2,1)} %get-tuple-element.87.left), channel_id=1, source_target_pairs={{0,128},{32,160},{64,192},{96,224},{128,0},{160,32},{192,64},{224,... | collective-permute-start | bytes 2359304 | tf_op jit(solution)/shard_map/ppermute | solution.py:20
  15.2 44.9 %collective-permute-start.4 = (bf16[384,1024]{1,0:T(8,128)(2,1)}, bf16[384,1024]{1,0:T(8,128)(2,1)}, u32[]{:S(2)}, u32[]{:S(2)}) collective-permute-start(bf16[384,1024]{1,0:T(8,128)(2,1)} %get-tuple-element.88.right), channel_id=1, source_target_pairs={{0,32},{32,64},{64,96},{96,0},{128,160},{160,192},{192,224},{224,1... | collective-permute-start | bytes 2359304 | tf_op jit(solution)/shard_map/ppermute | solution.py:20
  15.9 44.2 %collective-permute-start.2 = (bf16[384,1024]{1,0:T(8,128)(2,1)}, bf16[384,1024]{1,0:T(8,128)(2,1)S(1)}, u32[]{:S(2)}, u32[]{:S(2)}) collective-permute-start(bf16[384,1024]{1,0:T(8,128)(2,1)} %get-tuple-element.88.right), channel_id=1, source_target_pairs={{0,128},{32,160},{64,192},{96,224},{128,0},{160,32},{192,64},{224,... | collective-permute-start | bytes 2359304 | tf_op jit(solution)/shard_map/ppermute | solution.py:20
  16.7 43.1 %all-to-all-start = ((f32[32,3,128]{2,1,0:T(4,128)}), f32[32,3,128]{2,1,0:T(4,128)S(1)}, u32[]{:S(2)}, u32[]{:S(2)}) async-start(f32[32,3,128]{2,1,0:T(4,128)} %broadcast_in_dim.21), calls=%async_computation | async-start | bytes 131072 | tf_op jit(solution)/shard_map/cond/branch_1_fun/all_to_all | solution.py:29
  60.0 1.1 copy-start.5
  60.0 1.1 copy-start.7
  60.0 5.2 %copy-start.8 = (f32[8,48]{1,0:T(8,128)}, f32[8,48]{1,0:T(8,128)S(1)}, u32[]{:S(2)}) copy-start(f32[8,48]{1,0:T(8,128)S(1)} %get-tuple-element.90) | copy-start | bytes 4612
  60.0 5.2 %copy-start.6 = (bf16[8,120,48]{1,2,0:T(8,128)(2,1)S(1)}, bf16[8,120,48]{1,2,0:T(8,128)(2,1)}, u32[]{:S(2)}) copy-start(bf16[8,120,48]{1,2,0:T(8,128)(2,1)} %param.8) | copy-start | bytes 276484
  60.0 5.2 %copy-start.11 = (s32[3]{0:T(128)S(1)}, s32[3]{0:T(128)}, u32[]{:S(2)}) copy-start(s32[3]{0:T(128)} %copy-done.10) | copy-start | bytes 40
  61.0 46.1 %collective-permute-start.8 = (bf16[384,1024]{1,0:T(8,128)(2,1)}, bf16[384,1024]{1,0:T(8,128)(2,1)S(1)}, u32[]{:S(2)}, u32[]{:S(2)}) collective-permute-start(bf16[384,1024]{1,0:T(8,128)(2,1)} %broadcast_select_fusion), channel_id=1, source_target_pairs={{0,64},{32,96},{64,0},{96,32},{128,192},{160,224},{192,128},{224,1... | collective-permute-start | bytes 2359304 | tf_op jit(solution)/shard_map/ppermute | solution.py:20
  62.5 44.7 %collective-permute-start.6 = (bf16[384,1024]{1,0:T(8,128)(2,1)S(1)}, bf16[384,1024]{1,0:T(8,128)(2,1)S(1)}, u32[]{:S(2)}, u32[]{:S(2)}) collective-permute-start(bf16[384,1024]{1,0:T(8,128)(2,1)S(1)} %collective-permute-done.1.z_left), channel_id=1, source_target_pairs={{0,96},{32,0},{64,32},{96,64},{128,224},{160,128},{192,160},{224,1... | collective-permute-start | bytes 2359304 | tf_op jit(solution)/shard_map/ppermute | solution.py:20
  64.1 43.0 %collective-permute-start.7 = (bf16[384,1024]{1,0:T(8,128)(2,1)S(1)}, bf16[384,1024]{1,0:T(8,128)(2,1)}, u32[]{:S(2)}, u32[]{:S(2)}) collective-permute-start(bf16[384,1024]{1,0:T(8,128)(2,1)S(1)} %collective-permute-done.2.z_right), channel_id=1, source_target_pairs={{0,32},{32,64},{64,96},{96,0},{128,160},{160,192},{192,224},{224,1... | collective-permute-start | bytes 2359304 | tf_op jit(solution)/shard_map/ppermute | solution.py:20
  64.1 56.9 %collective-permute-start.10 = (f32[4,128,128]{2,1,0:T(8,128)}, f32[4,128,128]{2,1,0:T(8,128)}, u32[]{:S(2)}, u32[]{:S(2)}) collective-permute-start(f32[4,128,128]{2,1,0:T(8,128)} %copy-done.7), channel_id=1, source_target_pairs={{0,1},{1,0},{2,3},{3,2},{4,5},{5,4},{6,7},{7,6},{8,9},{9,8},{10,11... | collective-permute-start | bytes 786440 | tf_op jit(solution)/shard_map/ppermute | solution.py:24
  71.3 0.8 copy-start.2
  72.2 4.2 %collective-permute-start = (bf16[4,12,48,128]{3,2,1,0:T(8,128)(2,1)}, bf16[4,12,48,128]{3,2,1,0:T(8,128)(2,1)}, u32[]{:S(2)}, u32[]{:S(2)}) collective-permute-start(bf16[4,12,48,128]{3,2,1,0:T(8,128)(2,1)} %get-tuple-element.54), channel_id=1, source_target_pairs={{0,1},{1,0},{2,3},{3,2},{4,5},{5,4},{6,7},{7,6},{8,9},{9,8},{10,11... | collective-permute-start | bytes 1769480 | tf_op jit(solution)/shard_map/cond/branch_1_fun/ppermute | solution.py:24
  72.2 4.2 %copy-start.3 = (bf16[4,12,48,128]{3,2,1,0:T(8,128)(2,1)S(1)}, bf16[4,12,48,128]{3,2,1,0:T(8,128)(2,1)}, u32[]{:S(2)}) copy-start(bf16[4,12,48,128]{3,2,1,0:T(8,128)(2,1)} %copy-done.2) | copy-start | bytes 1769476 | tf_op jit(solution)/shard_map/cond
  78.4 14.0 %all-to-all-start.1 = ((bf16[4,576,128]{2,1,0:T(8,128)(2,1)}), bf16[4,576,128]{2,1,0:T(8,128)(2,1)}, u32[]{:S(2)}, u32[]{:S(2)}) async-start(bf16[4,576,128]{2,1,0:T(8,128)(2,1)} %bitcast.48), calls=%async_computation.1 | async-start | bytes 1179648 | tf_op jit(solution)/shard_map/cond/branch_1_fun/all_to_all | solution.py:269
  107.1 0.8 copy-start.4
  108.7 13.4 %all-to-all-start.3 = ((bf16[8,8,2048]{2,1,0:T(8,128)(2,1)}), bf16[8,8,2048]{2,1,0:T(8,128)(2,1)S(1)}, u32[]{:S(2)}, u32[]{:S(2)}) async-start(bf16[8,8,2048]{2,1,0:T(8,128)(2,1)} %broadcast_in_dim.32), calls=%async_computation.3 | async-start | bytes 524288 | tf_op jit(solution)/shard_map/all_to_all | solution.py:29
  117.5 0.8 copy-start
  118.3 7.9 %collective-permute-start.9 = (bf16[4,12,48,128]{3,2,1,0:T(8,128)(2,1)}, bf16[4,12,48,128]{3,2,1,0:T(8,128)(2,1)S(1)}, u32[]{:S(2)}, u32[]{:S(2)}) collective-permute-start(bf16[4,12,48,128]{3,2,1,0:T(8,128)(2,1)} %get-tuple-element.103), channel_id=1, source_target_pairs={{0,1},{1,0},{2,3},{3,2},{4,5},{5,4},{6,7},{7,6},{8,9},{9,8},{10,11... | collective-permute-start | bytes 1769480 | tf_op jit(solution)/shard_map/ppermute | solution.py:24
  122.1 4.2 %copy-start.1 = (bf16[4,12,48,128]{3,2,1,0:T(8,128)(2,1)S(1)}, bf16[4,12,48,128]{3,2,1,0:T(8,128)(2,1)}, u32[]{:S(2)}) copy-start(bf16[4,12,48,128]{3,2,1,0:T(8,128)(2,1)} %copy-done) | copy-start | bytes 1769476
  126.1 1.4 collective-permute-start.11
  128.7 16.4 %all-to-all-start.4 = ((bf16[4,832,128]{2,1,0:T(8,128)(2,1)}), bf16[4,832,128]{2,1,0:T(8,128)(2,1)S(1)}, u32[]{:S(2)}, u32[]{:S(2)}) async-start(bf16[4,832,128]{2,1,0:T(8,128)(2,1)} %pad_maximum_fusion.1), calls=%async_computation.4 | async-start | bytes 1703936 | tf_op jit(solution)/shard_map/all_to_all | solution.py:269
  146.1 11.6 %all-to-all-start.5 = ((bf16[8,144,128]{2,1,0:T(8,128)(2,1)}), bf16[8,144,128]{2,1,0:T(8,128)(2,1)S(1)}, u32[]{:S(2)}, u32[]{:S(2)}) async-start(bf16[8,144,128]{2,1,0:T(8,128)(2,1)} %bitcast.13), calls=%async_computation.5 | async-start | bytes 589824 | tf_op jit(solution)/shard_map/all_to_all | solution.py:341
  184.4 22.7 %copy-start.9 = (f32[8,48]{1,0:T(8,128)S(1)}, f32[8,48]{1,0:T(8,128)}, u32[]{:S(2)}) copy-start(f32[8,48]{1,0:T(8,128)} %copy-done.8) | copy-start | bytes 4612
  201.1 8.9 %collective-permute-start.12 = (bf16[4,4,352,128]{3,2,1,0:T(8,128)(2,1)S(1)}, bf16[4,4,352,128]{3,2,1,0:T(8,128)(2,1)S(1)}, u32[]{:S(2)}, u32[]{:S(2)}) collective-permute-start(bf16[4,4,352,128]{3,2,1,0:T(8,128)(2,1)S(1)} %all_to_all.45.own), channel_id=1, source_target_pairs={{0,1},{1,0},{2,3},{3,2},{4,5},{5,4},{6,7},{7,6},{8,9},{9,8},{10,11... | collective-permute-start | bytes 4325384 | tf_op jit(solution)/shard_map/ppermute | solution.py:24
  210.2 2.7 %copy-start.12 = (s32[3]{0:T(128)S(1)}, s32[3]{0:T(128)}, u32[]{:S(2)}) copy-start(s32[3]{0:T(128)} %copy-done.10) | copy-start | bytes 40

commit v4 on v3

--- a/solution.py
+++ b/solution.py
@@ -301,6 +301,7 @@
     def mode_work(fields, vectors, weights, scale, left, right, *near):
         keep, send = blocks_of(near_kernel, spot, left, right, *near)
         blocks = (keep.astype(F32) + swap_cores(send).astype(F32)).astype(BF16)
+        fields, blocks = barrier((fields, blocks))
         blocks = scatter_x(blocks.reshape(4, rows * 3 // 2, 128)).astype(BF16)
         projected = jnp.einsum("rmk,rmc->rkc", vectors, fields, preferred_element_type=F32)
         basis = (projected * lax.rsqrt(scale)[:, :, None]).astype(BF16).reshape(rows, cells)

time: 219 us -> 218 us (level)
    all_to_all x2, waiting for transfers between devices: 19.9 us -> 16.4 us  [scatter_x(): return sum_of(lax.all_to_all(parts, 'x', 0, 0, tiled=True))]
    ppermute x5, waiting for transfers between devices: 2.85 us -> 5.16 us  [swap_cores(): return lax.ppermute(x, 'core', [(0, 1), (1, 0)])]
  transfers between devices with their start and end apart: 18 -> 18, of which waited for: 6 -> 7; matrix products, arithmetic and copies ran while one was open for 7% -> 7% of each run, Pallas kernels for 10% -> 10%
where the time goes in v4:
time: 218 us; the launch traced here: 216 us
  blocking collectives  55.6 us (26%)
  waiting for transfers between devices  52 us (24%)
  starting transfers between devices  49.3 us (23%)
  Pallas kernels  33.6 us (15%)
  other arithmetic  12 us (6%)
  local copies, waits for them, and re-layouts  7.14 us (3%)
  matrix products  5.76 us (3%)
    all_to_all x2, blocking collectives, spread(): lax.all_to_all(jnp.broadcast_to(x[None], (n,) + x.shape), axes, 0, 0, til...  30 us
    all_to_all x2, waiting for transfers between devices, spread(): lax.all_to_all(jnp.broadcast_to(x[None], (n,) + x.shape), axes, 0, 0, til...  24.3 us
    all_to_all x2, starting transfers between devices, spread(): lax.all_to_all(jnp.broadcast_to(x[None], (n,) + x.shape), axes, 0, 0, til...  16.4 us
    all_to_all x2, waiting for transfers between devices, scatter_x(): return sum_of(lax.all_to_all(parts, 'x', 0, 0, tiled=True))  16.4 us
    all_to_all x1, blocking collectives, mode_work(): part = lax.all_to_all(part, RUNS, 0, 0, tiled=True)  13.7 us
    all_to_all x1, blocking collectives, per_device(): pieces = sum_of(lax.all_to_all(pieces, 'z_hi', 0, 0, tiled=True))  11.9 us
    pallas_call x2, Pallas kernels, blocks_of(): pl.pallas_call(kernel, in_specs=[pl.BlockSpec(memory_space=pltpu.SMEM)] +...  11.5 us
    ppermute x8, starting transfers between devices, send_to(): return lax.ppermute(x, RUNS, pairs)  9.94 us
  transfers between devices with their start and end apart: 18, of which 7 were waited for; matrix products, arithmetic and copies ran while one was open for 7% of the time, Pallas kernels for 10%

profile of v4, /device:TPU:1, one launch (start us, length us, event | category | flops | bytes accessed | tf_op | source)
XLA Modules:
  0.0 216.5 jit_solution(15322057867204212263)
XLA Ops:
  0.6 1.1 copy.40.vectors
  1.8 7.2 %shard_map.75 = (bf16[384,1024]{1,0:T(8,128)(2,1)}, bf16[384,1024]{1,0:T(8,128)(2,1)}, bf16[384,1024]{1,0:T(8,128)(2,1)S(1)}, f32[8,48,1]{2,1,0:T(8,128)S(1)}) custom-call(s32[3]{0:T(128)S(1)} %pad_add_fusion.spot, bf16[8,120,2048]{2,1,0:T(8,128)(2,1)} %second.1, bf16[8,120,48]{2,1,0:T(8,128)(2,1)S(1)} %copy.40.vectors), custom_call_target="tpu_custom_call" | custom-call | flops 188743680 | bytes 7864320 | tf_op jit(solution)/shard_map/pallas_call | solution.py:55
  9.0 3.7 %collective-permute-start.5 = (bf16[384,1024]{1,0:T(8,128)(2,1)S(1)}, bf16[384,1024]{1,0:T(8,128)(2,1)}, u32[]{:S(2)}, u32[]{:S(2)}) collective-permute-start(bf16[384,1024]{1,0:T(8,128)(2,1)S(1)} %get-tuple-element.91), channel_id=1, source_target_pairs={{0,64},{32,96},{64,0},{96,32},{128,192},{160,224},{192,128},{224,1... | collective-permute-start | bytes 2359304 | tf_op jit(solution)/shard_map/ppermute | solution.py:20
  12.8 0.8 collective-permute-start.3
  13.5 1.6 collective-permute-start.1
  15.9 44.1 %conditional.2 = (f32[8,48]{1,0:T(8,128)S(1)}, f32[4,128,128]{2,1,0:T(8,128)S(1)}, f32[4,128,128]{2,1,0:T(8,128)S(1)}) conditional(s32[]{:T(128)} %convert_element_type.88, () %tuple.32, (f32[8,48,1]{2,1,0:T(8,128)S(1)}, s32[]{:T(128)}, bf16[8,120,2048]{2,1,0:T(8,128)(2,1)}) %tuple.33), branch_computations={%region_0.0_spmd, %region_1.3_spmd} | conditional | flops 472002560 | bytes 5274698 | solution.py:276
  16.7 13.0 %all-to-all-start = ((f32[32,3,128]{2,1,0:T(4,128)}), f32[32,3,128]{2,1,0:T(4,128)S(1)}, u32[]{:S(2)}, u32[]{:S(2)}) async-start(f32[32,3,128]{2,1,0:T(4,128)} %broadcast_in_dim.21), calls=%async_computation | async-start | bytes 131072 | tf_op jit(solution)/shard_map/cond/branch_1_fun/all_to_all | solution.py:29
  29.7 5.8 %branch_1_fun.2 = f32[8,128,128]{2,1,0:T(8,128)S(1)} custom-call(bf16[8,120,2048]{2,1,0:T(8,128)(2,1)} %get-tuple-element.41.fields), custom_call_target="tpu_custom_call" | custom-call | flops 471859200 | bytes 3932160 | tf_op jit(solution)/shard_map/cond/branch_1_fun/pallas_call | solution.py:84
  35.6 24.3 %all-to-all-done = f32[32,3,128]{2,1,0:T(4,128)S(1)} async-done(((f32[32,3,128]{2,1,0:T(4,128)}), f32[32,3,128]{2,1,0:T(4,128)S(1)}, u32[]{:S(2)}, u32[]{:S(2)}) %all-to-all-start) | async-done | bytes 49184 | tf_op jit(solution)/shard_map/cond/branch_1_fun/all_to_all | solution.py:29
  60.0 1.0 broadcast_select_fusion
  61.0 1.4 collective-permute-start.8
  62.4 1.7 collective-permute-start.6
  64.1 1.0 collective-permute-start.10
  65.2 40.8 %conditional.3 = (bf16[384,2048]{1,0:T(8,128)(2,1)}, f32[8,8,2096]{2,1,0:T(8,128)S(1)}, bf16[576,128]{1,0:T(8,128)(2,1)S(1)}) conditional(s32[]{:T(128)} %convert_element_type.88, () %tuple.31, (s32[3]{0:T(128)S(1)}, bf16[384,1024]{1,0:T(8,128)(2,1)}, bf16[384,1024]{1,0:T(8,128)(2,1)}, bf16[384,1024]{1,0:T(8,128)(2,1)}, bf16[384,1024]{1,0:T(8,128)(2,1)}, ...), branch_computations={%region_3.4_spmd, %region_4.6_spmd} | conditional | flops 1651469312 | bytes 23621808 | solution.py:276
  65.2 6.2 %branch_1_fun.3 = (bf16[4,12,48,128]{3,2,1,0:T(8,128)(2,1)S(1)}, bf16[4,12,48,128]{3,2,1,0:T(8,128)(2,1)}) custom-call(s32[3]{0:T(128)S(1)} %get-tuple-element.43.spot, bf16[384,1024]{1,0:T(8,128)(2,1)} %get-tuple-element.44.left, bf16[384,1024]{1,0:T(8,128)(2,1)} %get-tuple-element.45.right, bf16[384,1024]{1,0:T(8,128)(2,1)} %get-tuple-element.46.down, ...), custom_call_target="tpu_custom_call" | custom-call | flops 1358954496 | bytes 4718592 | tf_op jit(solution)/shard_map/cond/branch_1_fun/pallas_call | solution.py:202
  71.3 0.8 copy-done.2
  72.2 2.3 %collective-permute-done = bf16[4,12,48,128]{3,2,1,0:T(8,128)(2,1)} collective-permute-done((bf16[4,12,48,128]{3,2,1,0:T(8,128)(2,1)}, bf16[4,12,48,128]{3,2,1,0:T(8,128)(2,1)}, u32[]{:S(2)}, u32[]{:S(2)}) %collective-permute-start) | collective-permute-done | bytes 589856 | tf_op jit(solution)/shard_map/cond/branch_1_fun/ppermute | solution.py:24
  74.5 2.2 %add_convert_fusion = bf16[4,12,48,128]{3,2,1,0:T(8,128)(2,1)} fusion(bf16[4,12,48,128]{3,2,1,0:T(8,128)(2,1)} %collective-permute-done, bf16[4,12,48,128]{3,2,1,0:T(8,128)(2,1)} %copy-done.2), kind=kLoop, calls=%fused_computation.1 | loop fusion | flops 1179648 | bytes 1769472 | tf_op jit(solution)/shard_map/cond/branch_1_fun/convert_element_type | solution.py:303
  76.7 4.3 %all-to-all-start.1 = ((bf16[4,576,128]{2,1,0:T(8,128)(2,1)}), bf16[4,576,128]{2,1,0:T(8,128)(2,1)}, u32[]{:S(2)}, u32[]{:S(2)}) async-start(bf16[4,576,128]{2,1,0:T(8,128)(2,1)} %bitcast.50), calls=%async_computation.1 | async-start | bytes 1179648 | tf_op jit(solution)/shard_map/cond/branch_1_fun/all_to_all | solution.py:269
  81.0 3.9 %multiply_convert_fusion = bf16[8,2048,48]{1,2,0:T(8,128)(2,1)} fusion(bf16[8,120,2048]{2,1,0:T(8,128)(2,1)} %get-tuple-element.51, bf16[8,120,48]{1,2,0:T(8,128)(2,1)S(1)} %get-tuple-element.52, f32[8,48]{1,0:T(8,128)S(1)} %rsqrt.26), kind=kOutput, calls=%fused_computation | convolution fusion | flops 190316544 | bytes 5598720 | tf_op jit(solution)/shard_map/cond/branch_1_fun/rmk,rmc->rkc/dot_general | solution.py:306
  85.0 1.8 fusion
  86.8 0.8 pad_maximum_fusion
  87.7 3.4 %all-to-all-done.1 = bf16[4,576,128]{2,1,0:T(8,128)(2,1)} async-done(((bf16[4,576,128]{2,1,0:T(8,128)(2,1)}), bf16[4,576,128]{2,1,0:T(8,128)(2,1)}, u32[]{:S(2)}, u32[]{:S(2)}) %all-to-all-start.1) | async-done | bytes 589856 | tf_op jit(solution)/shard_map/cond/branch_1_fun/all_to_all | solution.py:269
  91.1 1.2 reduce_sum.44
  92.3 13.7 %all_to_all.42 = f32[8,8,2096]{2,1,0:T(8,128)S(1)} all-to-all(f32[8,8,2096]{2,1,0:T(8,128)} %pad_maximum_fusion), channel_id=1, replica_groups=mesh['z_lo'=2,'y'=4,'x'=4,'z_hi'=4,'core'=2] {'z_lo','y'}, dimensions={0} | all-to-all | bytes 1073152 | tf_op jit(solution)/shard_map/cond/branch_1_fun/all_to_all | solution.py:311
  106.0 0.8 copy-done.3
  107.5 3.4 %all-to-all-start.3 = ((bf16[8,8,2048]{2,1,0:T(8,128)(2,1)}), bf16[8,8,2048]{2,1,0:T(8,128)(2,1)S(1)}, u32[]{:S(2)}, u32[]{:S(2)}) async-start(bf16[8,8,2048]{2,1,0:T(8,128)(2,1)} %broadcast_in_dim.32), calls=%async_computation.3 | async-start | bytes 524288 | tf_op jit(solution)/shard_map/all_to_all | solution.py:29
  110.9 5.3 %shard_map.76 = (bf16[4,12,48,128]{3,2,1,0:T(8,128)(2,1)S(1)}, bf16[4,12,48,128]{3,2,1,0:T(8,128)(2,1)}) custom-call(s32[3]{0:T(128)} %copy-done.9, bf16[384,1024]{1,0:T(8,128)(2,1)} %get-tuple-element.87.left, bf16[384,1024]{1,0:T(8,128)(2,1)} %get-tuple-element.88.right, bf16[384,1024]{1,0:T(8,128)(2,1)S(1)} %collective-permute-done.1.z_left, ...), custom_call_target="tpu_custom_call" | custom-call | flops 1358954496 | bytes 4718592 | tf_op jit(solution)/shard_map/pallas_call | solution.py:202
  116.3 0.8 copy-done
  117.1 2.5 %collective-permute-start.9 = (bf16[4,12,48,128]{3,2,1,0:T(8,128)(2,1)}, bf16[4,12,48,128]{3,2,1,0:T(8,128)(2,1)S(1)}, u32[]{:S(2)}, u32[]{:S(2)}) collective-permute-start(bf16[4,12,48,128]{3,2,1,0:T(8,128)(2,1)} %get-tuple-element.105), channel_id=1, source_target_pairs={{0,1},{1,0},{2,3},{3,2},{4,5},{5,4},{6,7},{7,6},{8,9},{9,8},{10,11... | collective-permute-start | bytes 1769480 | tf_op jit(solution)/shard_map/ppermute | solution.py:24
  119.7 1.1 add_convert_fusion.3
  120.7 4.0 %shard_map.77 = f32[4,128,128]{2,1,0:T(8,128)S(1)} custom-call(bf16[8,120,2048]{2,1,0:T(8,128)(2,1)} %second.1, bf16[8,120,2048]{2,1,0:T(8,128)(2,1)} %second.1, bf16[64,2048]{1,0:T(8,128)(2,1)S(1)} %bitcast.48), custom_call_target="tpu_custom_call" | custom-call | flops 251658240 | bytes 3932160 | tf_op jit(solution)/shard_map/pallas_call | solution.py:112
  125.1 1.1 collective-permute-done.11
  126.3 1.0 pad_maximum_fusion.1
  127.3 3.5 %all-to-all-start.4 = ((bf16[4,832,128]{2,1,0:T(8,128)(2,1)}), bf16[4,832,128]{2,1,0:T(8,128)(2,1)S(1)}, u32[]{:S(2)}, u32[]{:S(2)}) async-start(bf16[4,832,128]{2,1,0:T(8,128)(2,1)} %pad_maximum_fusion.1), calls=%async_computation.4 | async-start | bytes 1703936 | tf_op jit(solution)/shard_map/all_to_all | solution.py:269
  130.8 12.9 %all-to-all-done.4 = bf16[4,832,128]{2,1,0:T(8,128)(2,1)S(1)} async-done(((bf16[4,832,128]{2,1,0:T(8,128)(2,1)}), bf16[4,832,128]{2,1,0:T(8,128)(2,1)S(1)}, u32[]{:S(2)}, u32[]{:S(2)}) %all-to-all-start.4) | async-done | bytes 852000 | tf_op jit(solution)/shard_map/all_to_all | solution.py:269
  143.9 0.8 maximum_select_fusion
  144.7 5.3 %all-to-all-start.5 = ((bf16[8,144,128]{2,1,0:T(8,128)(2,1)}), bf16[8,144,128]{2,1,0:T(8,128)(2,1)S(1)}, u32[]{:S(2)}, u32[]{:S(2)}) async-start(bf16[8,144,128]{2,1,0:T(8,128)(2,1)} %bitcast.15), calls=%async_computation.5 | async-start | bytes 589824 | tf_op jit(solution)/shard_map/all_to_all | solution.py:342
  150.1 6.2 %all-to-all-done.5 = bf16[8,144,128]{2,1,0:T(8,128)(2,1)S(1)} async-done(((bf16[8,144,128]{2,1,0:T(8,128)(2,1)}), bf16[8,144,128]{2,1,0:T(8,128)(2,1)S(1)}, u32[]{:S(2)}, u32[]{:S(2)}) %all-to-all-start.5) | async-done | bytes 294944 | tf_op jit(solution)/shard_map/all_to_all | solution.py:342
  156.3 1.1 add_convert_fusion.2
  157.4 11.9 %all_to_all.43 = bf16[4,352,128]{2,1,0:T(8,128)(2,1)S(1)} all-to-all(bf16[4,352,128]{2,1,0:T(8,128)(2,1)S(1)} %pad_maximum_fusion.4), channel_id=1, replica_groups=mesh['z_lo'=2,'y'=4,'x'=4,'z_hi'=4,'core'=2] {'z_hi'}, dimensions={0} | all-to-all | bytes 720896 | tf_op jit(solution)/shard_map/all_to_all | solution.py:349
  169.5 13.4 %all_to_all.44 = bf16[4,352,128]{2,1,0:T(8,128)(2,1)S(1)} all-to-all(bf16[4,352,128]{2,1,0:T(8,128)(2,1)S(1)} %broadcast_in_dim.35), channel_id=1, replica_groups=mesh['z_lo'=2,'y'=4,'x'=4,'z_hi'=4,'core'=2] {'z_hi'}, dimensions={0} | all-to-all | bytes 720896 | tf_op jit(solution)/shard_map/all_to_all | solution.py:29
  183.1 16.6 %all_to_all.45.own = bf16[4,4,352,128]{3,2,1,0:T(8,128)(2,1)S(1)} all-to-all(bf16[4,4,352,128]{3,2,1,0:T(8,128)(2,1)S(1)} %broadcast_in_dim.36), channel_id=1, replica_groups=mesh['z_lo'=2,'y'=4,'x'=4,'z_hi'=4,'core'=2] {'x'}, dimensions={0} | all-to-all | bytes 2883584 | tf_op jit(solution)/shard_map/all_to_all | solution.py:29
  199.7 6.1 %collective-permute-start.12 = (bf16[4,4,352,128]{3,2,1,0:T(8,128)(2,1)S(1)}, bf16[4,4,352,128]{3,2,1,0:T(8,128)(2,1)S(1)}, u32[]{:S(2)}, u32[]{:S(2)}) collective-permute-start(bf16[4,4,352,128]{3,2,1,0:T(8,128)(2,1)S(1)} %all_to_all.45.own), channel_id=1, source_target_pairs={{0,1},{1,0},{2,3},{3,2},{4,5},{5,4},{6,7},{7,6},{8,9},{9,8},{10,11... | collective-permute-start | bytes 4325384 | tf_op jit(solution)/shard_map/ppermute | solution.py:24
  206.9 1.7 collective-permute-done.12.other
  209.8 0.8 fusion.5
  210.6 0.8 multiply_convert_fusion.1
  211.4 5.1 %shard_map.78 = f32[384,3072]{1,0:T(8,128)} custom-call(s32[3]{0:T(128)S(1)} %copy-done.11, bf16[4,4,352,128]{3,2,1,0:T(8,128)(2,1)S(1)} %all_to_all.45.own, bf16[4,4,352,128]{3,2,1,0:T(8,128)(2,1)S(1)} %collective-permute-done.12.other, f32[384,1]{1,0:T(8,128)S(1)} %div.43.row, f32[8,1,384]{2,1,0:T(1,128)S(1)} %rsqrt.34.col), custom_call_target="tpu_custom_call" | custom-call | tf_op jit(solution)/shard_map/pallas_call | solution.py:241
  (86 shorter events, 5.8 us)
Async XLA Ops:
  1.8 7.2 %copy-start.9 = (s32[3]{0:T(128)}, s32[3]{0:T(128)S(1)}, u32[]{:S(2)}) copy-start(s32[3]{0:T(128)S(1)} %pad_add_fusion.spot) | copy-start | bytes 40
  9.0 51.0 %collective-permute-start.5 = (bf16[384,1024]{1,0:T(8,128)(2,1)S(1)}, bf16[384,1024]{1,0:T(8,128)(2,1)}, u32[]{:S(2)}, u32[]{:S(2)}) collective-permute-start(bf16[384,1024]{1,0:T(8,128)(2,1)S(1)} %get-tuple-element.91), channel_id=1, source_target_pairs={{0,64},{32,96},{64,0},{96,32},{128,192},{160,224},{192,128},{224,1... | collective-permute-start | bytes 2359304 | tf_op jit(solution)/shard_map/ppermute | solution.py:20
  12.8 47.2 %collective-permute-start.3 = (bf16[384,1024]{1,0:T(8,128)(2,1)}, bf16[384,1024]{1,0:T(8,128)(2,1)}, u32[]{:S(2)}, u32[]{:S(2)}) collective-permute-start(bf16[384,1024]{1,0:T(8,128)(2,1)} %get-tuple-element.87.left), channel_id=1, source_target_pairs={{0,96},{32,0},{64,32},{96,64},{128,224},{160,128},{192,160},{224,1... | collective-permute-start | bytes 2359304 | tf_op jit(solution)/shard_map/ppermute | solution.py:20
  13.5 46.5 %collective-permute-start.1 = (bf16[384,1024]{1,0:T(8,128)(2,1)}, bf16[384,1024]{1,0:T(8,128)(2,1)S(1)}, u32[]{:S(2)}, u32[]{:S(2)}) collective-permute-start(bf16[384,1024]{1,0:T(8,128)(2,1)} %get-tuple-element.87.left), channel_id=1, source_target_pairs={{0,128},{32,160},{64,192},{96,224},{128,0},{160,32},{192,64},{224,... | collective-permute-start | bytes 2359304 | tf_op jit(solution)/shard_map/ppermute | solution.py:20
  15.2 44.9 %collective-permute-start.4 = (bf16[384,1024]{1,0:T(8,128)(2,1)}, bf16[384,1024]{1,0:T(8,128)(2,1)}, u32[]{:S(2)}, u32[]{:S(2)}) collective-permute-start(bf16[384,1024]{1,0:T(8,128)(2,1)} %get-tuple-element.88.right), channel_id=1, source_target_pairs={{0,32},{32,64},{64,96},{96,0},{128,160},{160,192},{192,224},{224,1... | collective-permute-start | bytes 2359304 | tf_op jit(solution)/shard_map/ppermute | solution.py:20
  15.9 44.2 %collective-permute-start.2 = (bf16[384,1024]{1,0:T(8,128)(2,1)}, bf16[384,1024]{1,0:T(8,128)(2,1)S(1)}, u32[]{:S(2)}, u32[]{:S(2)}) collective-permute-start(bf16[384,1024]{1,0:T(8,128)(2,1)} %get-tuple-element.88.right), channel_id=1, source_target_pairs={{0,128},{32,160},{64,192},{96,224},{128,0},{160,32},{192,64},{224,... | collective-permute-start | bytes 2359304 | tf_op jit(solution)/shard_map/ppermute | solution.py:20
  16.7 43.1 %all-to-all-start = ((f32[32,3,128]{2,1,0:T(4,128)}), f32[32,3,128]{2,1,0:T(4,128)S(1)}, u32[]{:S(2)}, u32[]{:S(2)}) async-start(f32[32,3,128]{2,1,0:T(4,128)} %broadcast_in_dim.21), calls=%async_computation | async-start | bytes 131072 | tf_op jit(solution)/shard_map/cond/branch_1_fun/all_to_all | solution.py:29
  59.9 1.1 copy-start.4
  59.9 1.1 copy-start.6
  60.0 5.2 %copy-start.7 = (f32[8,48]{1,0:T(8,128)}, f32[8,48]{1,0:T(8,128)S(1)}, u32[]{:S(2)}) copy-start(f32[8,48]{1,0:T(8,128)S(1)} %get-tuple-element.95) | copy-start | bytes 4612
  60.0 5.2 %copy-start.5 = (bf16[8,120,48]{1,2,0:T(8,128)(2,1)S(1)}, bf16[8,120,48]{1,2,0:T(8,128)(2,1)}, u32[]{:S(2)}) copy-start(bf16[8,120,48]{1,2,0:T(8,128)(2,1)} %param.8) | copy-start | bytes 276484
  60.0 5.2 %copy-start.10 = (s32[3]{0:T(128)S(1)}, s32[3]{0:T(128)}, u32[]{:S(2)}) copy-start(s32[3]{0:T(128)} %copy-done.9) | copy-start | bytes 40
  61.0 44.9 %collective-permute-start.8 = (bf16[384,1024]{1,0:T(8,128)(2,1)}, bf16[384,1024]{1,0:T(8,128)(2,1)S(1)}, u32[]{:S(2)}, u32[]{:S(2)}) collective-permute-start(bf16[384,1024]{1,0:T(8,128)(2,1)} %broadcast_select_fusion), channel_id=1, source_target_pairs={{0,64},{32,96},{64,0},{96,32},{128,192},{160,224},{192,128},{224,1... | collective-permute-start | bytes 2359304 | tf_op jit(solution)/shard_map/ppermute | solution.py:20
  62.4 43.5 %collective-permute-start.6 = (bf16[384,1024]{1,0:T(8,128)(2,1)S(1)}, bf16[384,1024]{1,0:T(8,128)(2,1)S(1)}, u32[]{:S(2)}, u32[]{:S(2)}) collective-permute-start(bf16[384,1024]{1,0:T(8,128)(2,1)S(1)} %collective-permute-done.1.z_left), channel_id=1, source_target_pairs={{0,96},{32,0},{64,32},{96,64},{128,224},{160,128},{192,160},{224,1... | collective-permute-start | bytes 2359304 | tf_op jit(solution)/shard_map/ppermute | solution.py:20
  64.1 41.9 %collective-permute-start.7 = (bf16[384,1024]{1,0:T(8,128)(2,1)S(1)}, bf16[384,1024]{1,0:T(8,128)(2,1)}, u32[]{:S(2)}, u32[]{:S(2)}) collective-permute-start(bf16[384,1024]{1,0:T(8,128)(2,1)S(1)} %collective-permute-done.2.z_right), channel_id=1, source_target_pairs={{0,32},{32,64},{64,96},{96,0},{128,160},{160,192},{192,224},{224,1... | collective-permute-start | bytes 2359304 | tf_op jit(solution)/shard_map/ppermute | solution.py:20
  64.1 55.5 %collective-permute-start.10 = (f32[4,128,128]{2,1,0:T(8,128)}, f32[4,128,128]{2,1,0:T(8,128)}, u32[]{:S(2)}, u32[]{:S(2)}) collective-permute-start(f32[4,128,128]{2,1,0:T(8,128)} %copy-done.6), channel_id=1, source_target_pairs={{0,1},{1,0},{2,3},{3,2},{4,5},{5,4},{6,7},{7,6},{8,9},{9,8},{10,11... | collective-permute-start | bytes 786440 | tf_op jit(solution)/shard_map/ppermute | solution.py:24
  71.3 0.8 copy-start.2
  72.1 2.3 %collective-permute-start = (bf16[4,12,48,128]{3,2,1,0:T(8,128)(2,1)}, bf16[4,12,48,128]{3,2,1,0:T(8,128)(2,1)}, u32[]{:S(2)}, u32[]{:S(2)}) collective-permute-start(bf16[4,12,48,128]{3,2,1,0:T(8,128)(2,1)} %get-tuple-element.50), channel_id=1, source_target_pairs={{0,1},{1,0},{2,3},{3,2},{4,5},{5,4},{6,7},{7,6},{8,9},{9,8},{10,11... | collective-permute-start | bytes 1769480 | tf_op jit(solution)/shard_map/cond/branch_1_fun/ppermute | solution.py:24
  76.7 14.4 %all-to-all-start.1 = ((bf16[4,576,128]{2,1,0:T(8,128)(2,1)}), bf16[4,576,128]{2,1,0:T(8,128)(2,1)}, u32[]{:S(2)}, u32[]{:S(2)}) async-start(bf16[4,576,128]{2,1,0:T(8,128)(2,1)} %bitcast.50), calls=%async_computation.1 | async-start | bytes 1179648 | tf_op jit(solution)/shard_map/cond/branch_1_fun/all_to_all | solution.py:269
  106.0 0.8 copy-start.3
  107.5 13.2 %all-to-all-start.3 = ((bf16[8,8,2048]{2,1,0:T(8,128)(2,1)}), bf16[8,8,2048]{2,1,0:T(8,128)(2,1)S(1)}, u32[]{:S(2)}, u32[]{:S(2)}) async-start(bf16[8,8,2048]{2,1,0:T(8,128)(2,1)} %broadcast_in_dim.32), calls=%async_computation.3 | async-start | bytes 524288 | tf_op jit(solution)/shard_map/all_to_all | solution.py:29
  116.3 0.8 copy-start
  117.1 7.8 %collective-permute-start.9 = (bf16[4,12,48,128]{3,2,1,0:T(8,128)(2,1)}, bf16[4,12,48,128]{3,2,1,0:T(8,128)(2,1)S(1)}, u32[]{:S(2)}, u32[]{:S(2)}) collective-permute-start(bf16[4,12,48,128]{3,2,1,0:T(8,128)(2,1)} %get-tuple-element.105), channel_id=1, source_target_pairs={{0,1},{1,0},{2,3},{3,2},{4,5},{5,4},{6,7},{7,6},{8,9},{9,8},{10,11... | collective-permute-start | bytes 1769480 | tf_op jit(solution)/shard_map/ppermute | solution.py:24
  120.7 4.2 %copy-start.1 = (bf16[4,12,48,128]{3,2,1,0:T(8,128)(2,1)S(1)}, bf16[4,12,48,128]{3,2,1,0:T(8,128)(2,1)}, u32[]{:S(2)}) copy-start(bf16[4,12,48,128]{3,2,1,0:T(8,128)(2,1)} %copy-done) | copy-start | bytes 1769476
  124.8 1.4 collective-permute-start.11
  127.3 16.4 %all-to-all-start.4 = ((bf16[4,832,128]{2,1,0:T(8,128)(2,1)}), bf16[4,832,128]{2,1,0:T(8,128)(2,1)S(1)}, u32[]{:S(2)}, u32[]{:S(2)}) async-start(bf16[4,832,128]{2,1,0:T(8,128)(2,1)} %pad_maximum_fusion.1), calls=%async_computation.4 | async-start | bytes 1703936 | tf_op jit(solution)/shard_map/all_to_all | solution.py:269
  144.7 11.5 %all-to-all-start.5 = ((bf16[8,144,128]{2,1,0:T(8,128)(2,1)}), bf16[8,144,128]{2,1,0:T(8,128)(2,1)S(1)}, u32[]{:S(2)}, u32[]{:S(2)}) async-start(bf16[8,144,128]{2,1,0:T(8,128)(2,1)} %bitcast.15), calls=%async_computation.5 | async-start | bytes 589824 | tf_op jit(solution)/shard_map/all_to_all | solution.py:342
  183.0 22.7 %copy-start.8 = (f32[8,48]{1,0:T(8,128)S(1)}, f32[8,48]{1,0:T(8,128)}, u32[]{:S(2)}) copy-start(f32[8,48]{1,0:T(8,128)} %copy-done.7) | copy-start | bytes 4612
  199.7 8.9 %collective-permute-start.12 = (bf16[4,4,352,128]{3,2,1,0:T(8,128)(2,1)S(1)}, bf16[4,4,352,128]{3,2,1,0:T(8,128)(2,1)S(1)}, u32[]{:S(2)}, u32[]{:S(2)}) collective-permute-start(bf16[4,4,352,128]{3,2,1,0:T(8,128)(2,1)S(1)} %all_to_all.45.own), channel_id=1, source_target_pairs={{0,1},{1,0},{2,3},{3,2},{4,5},{5,4},{6,7},{7,6},{8,9},{9,8},{10,11... | collective-permute-start | bytes 4325384 | tf_op jit(solution)/shard_map/ppermute | solution.py:24
  208.8 2.7 %copy-start.11 = (s32[3]{0:T(128)S(1)}, s32[3]{0:T(128)}, u32[]{:S(2)}) copy-start(s32[3]{0:T(128)} %copy-done.9) | copy-start | bytes 40
